TPU v7x, 32 devices: a whole 2x2x4 slice. The times are simulated.
32 devices in a mesh: ctx: 8 (over y, x, core), tp: 4 (over z).
Axes of the slice: x: 2, y: 2, z: 4, core: 2. Of those that a mesh axis runs over, the one named last changes fastest.
Arguments:
- queries: bfloat16 [2048, 2048], P('ctx', 'tp'), may hold values from -24 to 24
- key_heads: bfloat16 [2048, 4, 128], P('ctx'), may hold values from -6 to 6
- head_values: bfloat16 [2048, 4, 128], P('ctx'), may hold values from -6 to 6
- hidden: bfloat16 [2048, 4096], P('ctx'), may hold values from -0.59765625 to 0.59765625
- out_proj: bfloat16 [2048, 4096], P('tp'), may hold values from -0.125 to 0.125
- norm_gain: float32 [4096], replicated, may hold values from 0.25 to 1.75
- x_proj: bfloat16 [4096, 4096], P('ctx', 'tp'), may hold values from -0.046875 to 0.046875
- bc_proj: bfloat16 [4096, 4, 256], P('ctx'), may hold values from -0.09375 to 0.09375
- dt_proj: bfloat16 [4096, 64], P('ctx', 'tp'), may hold values from -0.09375 to 0.09375
- dt_bias: float32 [64], P('tp'), may hold values from -12 to 0
- decay_log: float32 [64], P('tp'), may hold values from -10 to 3
- skip_gain: float32 [64], P('tp'), may hold values from 0.5 to 1.5
Outputs:
- residual_out: bfloat16 [2048, 4096], P('ctx', 'tp')
- mamba_out: bfloat16 [2048, 4096], P('ctx', 'tp')
All inputs are finite; a program needn't handle non-finite values.
Results may differ from a plain program's by a relative error of at most 0.034.
Values may be sent and summed in bfloat16 or wider, within the bound.
A program may use at most 64 MiB of HBM per device.

v0:
```python
import math

import jax
import jax.numpy as jnp
from jax import lax
from jax.sharding import PartitionSpec as P


def prefix(value, axis, join, neutral, backward):
    count, mine = (lax.axis_size(axis), lax.axis_index(axis))
    pieces = jax.tree.map(lambda part: lax.all_gather(part, axis), value)
    if backward:
        pieces = jax.tree.map(lambda part: part[::-1], pieces)
        mine = count - 1 - mine
    so_far = jax.tree.map(
        lambda part, zero: jnp.full_like(part, 0) + jnp.asarray(zero, part.dtype), value, neutral
    )

    def lap(position, so_far):
        longer = join(so_far, jax.tree.map(lambda part: part[position], pieces))
        return jax.tree.map(lambda new, old: jnp.where(position < mine, new, old), longer, so_far)

    return lax.fori_loop(0, count - 1, lap, so_far)


def chain(earlier, later):
    return (earlier[0] * later[0], later[0][..., None, None] * earlier[1] + later[1])


def block_positions(rows, tok_dev, n_ctx):
    half = tok_dev // 2
    device = rows // tok_dev
    within = rows % tok_dev
    block = jnp.where(within < half, device, 2 * n_ctx - 1 - device)
    return block * half + within % half


def split_product(form, wide, narrow):
    upper = wide.astype(jnp.bfloat16)
    lower = (wide - upper.astype(jnp.float32)).astype(jnp.bfloat16)
    first_term = jnp.einsum(form, upper, narrow, preferred_element_type=jnp.float32)
    return first_term + jnp.einsum(form, lower, narrow, preferred_element_type=jnp.float32)


def body(
    queries,
    key_heads,
    head_values,
    hidden,
    out_proj,
    norm_gain,
    x_proj,
    bc_proj,
    dt_proj,
    dt_bias,
    decay_log,
    skip_gain,
):
    tok_dev = queries.shape[0]
    half = tok_dev // 2
    n_ctx = lax.axis_size("ctx")
    n_tp = lax.axis_size("tp")
    ctx_index = lax.axis_index("ctx")
    tp_index = lax.axis_index("tp")
    head_dim = key_heads.shape[2]
    kv_total = key_heads.shape[1]
    q_local = queries.shape[1] // head_dim
    group = q_local * n_tp // kv_total
    kv_local = max(1, q_local // group)
    per_kv = q_local // kv_local
    kv_start = tp_index * q_local // group
    keys_mine = lax.dynamic_slice_in_dim(key_heads, kv_start, kv_local, 1)
    values_mine = lax.dynamic_slice_in_dim(head_values, kv_start, kv_local, 1)
    query_pos = block_positions(
        ctx_index * tok_dev + jnp.arange(tok_dev, dtype=jnp.int32), tok_dev, n_ctx
    )
    shaped_q = queries.reshape(tok_dev, kv_local, per_kv, head_dim)
    root_dim = math.sqrt(head_dim)
    start_max = jnp.full((kv_local, per_kv, tok_dev), -1e30, jnp.float32)
    run_max = start_max
    key_piece = lax.all_gather(keys_mine, "ctx", axis=0, tiled=True)
    value_piece = lax.all_gather(values_mine, "ctx", axis=0, tiled=True)
    count = key_piece.shape[0]
    key_pos = block_positions(jnp.arange(count, dtype=jnp.int32), tok_dev, n_ctx)
    scores = (
        jnp.einsum("qgjd,kgd->gjqk", shaped_q, key_piece, preferred_element_type=jnp.float32)
        / root_dim
    )
    allowed = key_pos[None, :] <= query_pos[:, None]
    piece_max = jnp.max(jnp.where(allowed, scores, -1e30), axis=-1)
    new_max = jnp.maximum(run_max, piece_max)
    weights = jnp.where(allowed, jnp.exp(scores - new_max[..., None]), 0.0)
    run_sum = jnp.sum(weights, axis=-1)
    update = jnp.einsum(
        "gjqk,kgd->gjqd",
        weights.astype(jnp.bfloat16),
        value_piece,
        preferred_element_type=jnp.float32,
    )
    accum = update
    run_max, run_sum, accum = (new_max, run_sum, accum)
    attended = (
        jnp.transpose(accum / run_sum[..., None], (2, 0, 1, 3))
        .reshape(tok_dev, q_local * head_dim)
        .astype(jnp.bfloat16)
    )
    head_part = jnp.dot(attended, out_proj, preferred_element_type=jnp.float32)
    slice_width = hidden.shape[1] // n_tp
    attention_sum = lax.psum(head_part.astype(jnp.bfloat16), "tp").astype(jnp.float32)
    residual = (hidden.astype(jnp.float32) + attention_sum).astype(jnp.bfloat16)
    residual_out = lax.dynamic_slice_in_dim(residual, tp_index * slice_width, slice_width, 1)
    as_float = residual.astype(jnp.float32)
    mean_square = jnp.mean(as_float * as_float, axis=-1, keepdims=True)
    normed = (as_float * lax.rsqrt(mean_square + 1e-05) * norm_gain).astype(jnp.bfloat16)
    m_local = skip_gain.shape[0]
    state_size = bc_proj.shape[2] // 2
    groups_all = bc_proj.shape[1]
    per_group = m_local * n_tp // groups_all
    g_local = max(1, m_local // per_group)
    heads_each = m_local // g_local
    g_start = tp_index * m_local // per_group
    head_width = x_proj.shape[1] // m_local
    bc_mine = lax.dynamic_slice_in_dim(bc_proj, g_start, g_local, 1).reshape(
        bc_proj.shape[0], g_local * 2 * state_size
    )
    sum_x = jnp.dot(
        normed,
        lax.all_gather(x_proj, "ctx", axis=0, tiled=True),
        preferred_element_type=jnp.float32,
    )
    sum_bc = jnp.dot(
        normed,
        lax.all_gather(bc_mine, "ctx", axis=0, tiled=True),
        preferred_element_type=jnp.float32,
    )
    sum_dt = jnp.dot(
        normed,
        lax.all_gather(dt_proj, "ctx", axis=0, tiled=True),
        preferred_element_type=jnp.float32,
    )
    inputs_low = sum_x.astype(jnp.bfloat16).reshape(2, half, g_local, heads_each, head_width)
    inputs = inputs_low.astype(jnp.float32)
    bc_round = sum_bc.astype(jnp.bfloat16).reshape(2, half, g_local, 2 * state_size)
    b_low = bc_round[..., :state_size]
    c_low = bc_round[..., state_size:]
    steps = jax.nn.softplus(sum_dt + dt_bias).reshape(2, half, g_local, heads_each)
    rates = -jnp.exp(decay_log).reshape(g_local, heads_each)
    cumul = jnp.transpose(jnp.cumsum(steps * rates, axis=1), (0, 2, 3, 1))
    step_rows = jnp.transpose(steps, (0, 2, 3, 1))
    gram = jnp.einsum("ckgn,csgn->cgks", c_low, b_low, preferred_element_type=jnp.float32)
    places = jnp.arange(half, dtype=jnp.int32)
    causal = places[None, :] <= places[:, None]
    gaps = cumul[..., :, None] - cumul[..., None, :]
    decay = jnp.where(causal, jnp.exp(jnp.where(causal, gaps, 0.0)), 0.0)
    mixing = gram[:, :, None] * decay * step_rows[..., None, :]
    inner = split_product("cgjks,csgjp->ckgjp", mixing, inputs_low)
    last = cumul[..., -1]
    tail = jnp.exp(last[..., None] - cumul) * step_rows
    weighted = jnp.transpose(tail, (0, 3, 1, 2))[..., None] * inputs
    block_state = split_product("csgjp,csgn->cgjpn", weighted, b_low)
    block_decay = jnp.exp(last)
    first = (block_decay[0], block_state[0])
    second = (block_decay[1], block_state[1])
    unit = (jnp.ones_like(first[0]), jnp.zeros_like(first[1]))
    before = prefix(first, "ctx", chain, unit, False)
    last_device = ctx_index == n_ctx - 1
    through = chain(before, first)
    joined = chain(through, second)
    sent = (
        jnp.where(last_device, joined[0], second[0]),
        jnp.where(last_device, joined[1], second[1]),
    )
    after = prefix(sent, "ctx", chain, unit, True)
    second_in = jnp.where(last_device, through[1], after[1])
    entering = jnp.stack([before[1], second_in])
    carried = jnp.transpose(jnp.exp(cumul), (0, 3, 1, 2))[..., None] * split_product(
        "cgjpn,ckgn->ckgjp", entering, c_low
    )
    output = inner + carried + skip_gain.reshape(g_local, heads_each)[:, :, None] * inputs
    mamba_out = output.reshape(tok_dev, m_local * head_width).astype(jnp.bfloat16)
    return (residual_out, mamba_out)


def solution(mesh):
    placed = (
        P("ctx", "tp"),
        P("ctx", None, None),
        P("ctx", None, None),
        P("ctx", None),
        P("tp", None),
        P(),
        P("ctx", "tp"),
        P("ctx", None, None),
        P("ctx", "tp"),
        P("tp"),
        P("tp"),
        P("tp"),
    )
    return jax.shard_map(
        body,
        mesh=mesh,
        in_specs=placed,
        out_specs=(P("ctx", "tp"), P("ctx", "tp")),
        check_vma=False,
    )
```

profile of v0, /device:TPU:1, one launch (start us, length us, event | category | flops | bytes accessed | tf_op | source)
XLA Modules:
  0.0 260.2 jit_solution(18395014587411484655)
XLA Ops:
  9.3 11.2 %all_gather.33 = bf16[2048,1,128]{2,0,1:T(8,128)(2,1)S(1)} all-gather(bf16[256,1,128]{2,0,1:T(8,128)(2,1)S(1)} %copy.141), channel_id=1, replica_groups=mesh['ctx'=8,'tp'=4] {'ctx'}, dimensions={0}, use_global_device_ids=true | all-gather | bytes 589824 | tf_op jit(solution)/shard_map/all_gather | solution.py:81
  21.0 5.7 %fusion.3 = (f32[4,256]{1,0:T(4,128)S(1)}, f32[2048,256,4]{1,0,2:T(8,128)}) fusion(pred[256,2048]{0,1:T(8,128)(4,1)S(1)} %broadcast_compare_fusion, bf16[2048,1,128]{2,0,1:T(8,128)(2,1)S(1)} %all_gather.33, bf16[256,512]{1,0:T(8,128)(2,1)} %param.16), kind=kOutput, calls=%fused_computation.11 | convolution fusion | flops 543161344 | bytes 9703424 | tf_op jit(solution)/shard_map/qgjd,kgd->gjqk/dot_general | solution.py:86
  26.9 11.2 %all_gather.34 = bf16[2048,1,128]{0,2,1:T(8,128)(2,1)S(1)} all-gather(bf16[256,1,128]{0,2,1:T(8,128)(2,1)S(1)} %copy.140), channel_id=1, replica_groups=mesh['ctx'=8,'tp'=4] {'ctx'}, dimensions={0}, use_global_device_ids=true | all-gather | bytes 589824 | tf_op jit(solution)/shard_map/all_gather | solution.py:82
  38.2 4.5 %fusion.6 = f32[4,256]{1,0:T(4,128)S(1)} fusion(f32[2048,256,4]{1,0,2:T(8,128)} %get-tuple-element.343, f32[4,256]{1,0:T(4,128)S(1)} %broadcast_maximum_fusion, pred[256,2048]{0,1:T(8,128)(4,1)S(1)} %broadcast_compare_fusion), kind=kLoop, calls=%fused_computation.14 | loop fusion | flops 8387584 | bytes 8921088 | tf_op jit(solution)/shard_map/reduce_sum | solution.py:93
  42.7 1.3 copy-done.1
  44.0 1.8 fusion.36
  46.2 2.6 %convolution_convert_fusion = bf16[256,4096]{1,0:T(8,128)(2,1)} fusion(bf16[256,512]{0,1:T(8,128)(2,1)S(1)} %bitcast.182, bf16[512,4096]{1,0:T(8,128)(2,1)S(1)} %copy-done.5), kind=kOutput, calls=%fused_computation.18 | convolution fusion | flops 1074790400 | bytes 6553600 | tf_op jit(solution)/shard_map/dot_general | solution.py:107
  50.9 8.4 %all_gather.37 = bf16[4096,16]{0,1:T(8,128)(2,1)S(1)} all-gather(bf16[512,16]{0,1:T(8,128)(2,1)S(1)} %copy-done.9), channel_id=1, replica_groups=mesh['ctx'=8,'tp'=4] {'ctx'}, dimensions={0}, use_global_device_ids=true | all-gather | bytes 147456 | tf_op jit(solution)/shard_map/all_gather | solution.py:138
  59.4 75.9 %all-reduce.2.cloned.1.call-done = bf16[256,4096]{1,0:T(8,128)(2,1)} async-done(((bf16[256,4096]{1,0:T(8,128)(2,1)}), bf16[256,4096]{1,0:T(8,128)(2,1)}) %all-reduce.2.cloned.1.call-update) | async-done | bytes 2097168 | tf_op jit(solution)/shard_map/psum | solution.py:109
  135.3 3.2 %fusion.8 = (f32[256]{0:T(256)S(1)}, bf16[256,4096]{1,0:T(8,128)(2,1)S(1)}) fusion(bf16[256,4096]{1,0:T(8,128)(2,1)} %all-reduce.2.cloned.1.call-done, bf16[256,4096]{1,0:T(8,128)(2,1)} %param.19), kind=kLoop, calls=%fused_computation.19 | loop fusion | flops 7339776 | bytes 6292480 | tf_op jit(solution)/shard_map/reduce_sum | solution.py:113
  139.7 2.4 fusion.24
  142.1 6.6 %convolution_convert_fusion.1 = bf16[256,1024]{1,0:T(8,128)(2,1)} fusion(bf16[4096,1024]{1,0:T(8,128)(2,1)} %all-gather.11.cloned.1.call-done, bf16[256,4096]{1,0:T(8,128)(2,1)S(1)} %get-tuple-element.334, f32[4096]{0:T(1024)S(1)} %copy-done.11, f32[256]{0:T(256)S(1)} %add_rsqrt_fusion), kind=kOutput, calls=%fused_computation.41 | convolution fusion | flops 2151940096 | bytes 11027456 | tf_op jit(solution)/shard_map/dot_general | solution.py:126
  148.7 1.8 reshape.371
  152.9 9.2 %all-gather.1 = f32[8,1,16,1]{2,3,1,0:T(1,128)S(1)} all-gather(f32[1,1,16,1]{2,3,1,0:T(1,128)S(1)} %get-tuple-element.341), channel_id=3, replica_groups=mesh['ctx'=8,'tp'=4] {'ctx'}, dimensions={0}, use_global_device_ids=true | all-gather | bytes 576 | tf_op jit(solution)/shard_map/all_gather | solution.py:11
  162.1 26.7 %all-gather.15.cloned.1.call-done = f32[8,16,64,128]{3,2,1,0:T(8,128)} async-done(((f32[1,16,64,128]{3,2,1,0:T(8,128)}), f32[8,16,64,128]{3,2,1,0:T(8,128)}) %all-gather.15.cloned.1.call-update) | async-done | bytes 4194320 | tf_op jit(solution)/shard_map/all_gather | solution.py:11
  188.8 8.6 %while.30 = (s32[]{:T(128)}, f32[1,16]{1,0:T(1,128)S(1)}, f32[1,16,64,128]{3,2,1,0:T(8,128)S(1)}, s32[]{:T(128)}, f32[8,1,16]{2,1,0:T(1,128)S(1)}, /*index=5*/f32[8,1,16,64,128]{4,3,2,1,0:T(8,128)}, s32[]{:T(128)}, s32[]{:T(128)}) while((s32[]{:T(128)}, f32[1,16]{1,0:T(1,128)S(1)}, f32[1,16,64,128]{3,2,1,0:T(8,128)S(1)}, ...), condition=%wide.region_6.7_spmd.clone, body=%wide.region_5.6_spmd.clone.sunk | while | flops 524340 | bytes 1573375 | solution.py:23
  190.1 1.2 fusion.108
  192.5 1.2 fusion.108
  193.8 1.2 fusion.108
  195.0 1.2 fusion.108
  196.2 1.2 fusion.108
  198.5 1.9 constant_dynamic-slice_fusion.2
  200.6 2.8 %reshape.369 = f32[2,128,1,16,64]{4,3,1,0,2:T(8,128)} reshape(bf16[256,1024]{1,0:T(8,128)(2,1)} %convolution_convert_fusion.1) | data formatting | bytes 1572864 | tf_op jit(solution)/shard_map/convert_element_type | solution.py:142
  203.4 3.4 %copy.128 = f32[2,128,1,16,64]{1,4,3,0,2:T(8,128)} copy(f32[2,128,1,16,64]{4,3,1,0,2:T(8,128)} %reshape.369) | data formatting | bytes 2097152 | tf_op jit(solution)/shard_map/convert_element_type | solution.py:142
  206.7 2.1 fusion.40
  208.9 2.0 fusion.18
  210.9 9.0 %all-gather.5 = f32[8,1,16]{2,1,0:T(1,128)S(1)} all-gather(f32[1,1,16]{2,1,0:T(1,128)S(1)} %fusion.85), channel_id=5, replica_groups=mesh['ctx'=8,'tp'=4] {'ctx'}, dimensions={0}, use_global_device_ids=true | all-gather | bytes 576 | tf_op jit(solution)/shard_map/all_gather | solution.py:11
  219.9 15.2 %all-gather.17.cloned.1.call-done = f32[8,16,64,128]{3,2,1,0:T(8,128)} async-done(((f32[1,16,64,128]{3,2,1,0:T(8,128)}), f32[8,16,64,128]{3,2,1,0:T(8,128)}) %all-gather.17.cloned.1.call-update) | async-done | bytes 4194320 | tf_op jit(solution)/shard_map/all_gather | solution.py:11
  235.1 4.8 %reverse_bitcast_fusion = f32[8,1,16,64,128]{4,3,2,1,0:T(8,128)} fusion(f32[8,16,64,128]{3,2,1,0:T(8,128)} %all-gather.17.cloned.1.call-done), kind=kLoop, calls=%fused_computation.23 | loop fusion | bytes 8388608
  239.8 8.5 %while.31 = (s32[]{:T(128)}, f32[1,16,64,128]{3,2,1,0:T(8,128)S(1)}, s32[]{:T(128)}, f32[8,1,16]{2,1,0:T(1,128)S(1)}, f32[8,1,16,64,128]{4,3,2,1,0:T(8,128)}, /*index=5*/s32[]{:T(128)}, s32[]{:T(128)}) while((s32[]{:T(128)}, f32[1,16,64,128]{3,2,1,0:T(8,128)S(1)}, s32[]{:T(128)}, f32[8,1,16]{2,1,0:T(1,128)S(1)}, ...), condition=%wide.region_8.9_spmd.clone, body=%wide.region_7.8_spmd.clone.sunk | while | flops 524292 | bytes 1573169 | solution.py:23
  239.9 1.2 fusion.109
  251.1 1.5 reshape.370
  (106 shorter events, 21.4 us)
Async XLA Ops:
  8.0 40.9 %copy-start = (bf16[512,4,256]{2,1,0:T(4,128)(2,1)S(1)}, bf16[512,4,256]{2,1,0:T(4,128)(2,1)}, u32[]{:S(2)}) copy-start(bf16[512,4,256]{2,1,0:T(4,128)(2,1)} %param.23) | copy-start | bytes 3145732
  8.0 127.3 %all-reduce.2.cloned.1.call-start = ((), (), s32[]{:S(2)}) async-start(), calls=%async_computation | async-start | bytes 4194304 | tf_op jit(solution)/shard_map/psum | solution.py:109
  21.0 5.7 %copy-start.8 = (bf16[256,4,128]{2,1,0:T(4,128)(2,1)S(1)}, bf16[256,4,128]{2,1,0:T(4,128)(2,1)}, u32[]{:S(2)}) copy-start(bf16[256,4,128]{2,1,0:T(4,128)(2,1)} %param.18) | copy-start | bytes 786436
  38.2 5.8 %copy-start.1 = (f32[2048,256,4]{1,0,2:T(8,128)S(1)}, f32[2048,256,4]{1,0,2:T(8,128)}, u32[]{:S(2)}) copy-start(f32[2048,256,4]{1,0,2:T(8,128)} %get-tuple-element.343) | copy-start | bytes 25165828
  44.0 2.2 copy-start.5
  48.8 2.1 copy-start.9
  48.8 10.5 %copy-start.12 = (f32[16]{0:T(128)S(1)}, f32[16]{0:T(128)}, u32[]{:S(2)}) copy-start(f32[16]{0:T(128)} %param.26) | copy-start | bytes 196
  48.9 90.9 %all-gather.13.cloned.1.call-start = ((), (), s32[]{:S(2)}) async-start(), calls=%async_computation.2 | async-start | bytes 2359296 | tf_op jit(solution)/shard_map/all_gather | solution.py:133
  49.5 89.0 %copy-start.11 = (f32[4096]{0:T(1024)S(1)}, f32[4096]{0:T(1024)}, u32[]{:S(2)}) copy-start(f32[4096]{0:T(1024)} %param.21) | copy-start | bytes 49156
  49.5 89.0 %copy-start.13 = (f32[16]{0:T(128)S(1)}, f32[16]{0:T(128)}, u32[]{:S(2)}) copy-start(f32[16]{0:T(128)} %param.25) | copy-start | bytes 196
  50.3 91.8 %all-gather.11.cloned.1.call-start = ((), (), s32[]{:S(2)}) async-start(), calls=%async_computation.1 | async-start | bytes 9437184 | tf_op jit(solution)/shard_map/all_gather | solution.py:128
  50.9 137.9 %all-gather.15.cloned.1.call-start = ((), (), s32[]{:S(2)}) async-start(), calls=%async_computation.3 | async-start | bytes 4718592 | tf_op jit(solution)/shard_map/all_gather | solution.py:11
  138.5 3.7 %copy-start.6 = (bf16[256,4096]{1,0:T(8,128)(2,1)}, bf16[256,4096]{1,0:T(8,128)(2,1)S(1)}, u32[]{:S(2)}) copy-start(bf16[256,4096]{1,0:T(8,128)(2,1)S(1)} %get-tuple-element.334) | copy-start | bytes 6291460
  151.3 1.5 copy-start.2
  152.8 82.3 %all-gather.17.cloned.1.call-start = ((), (), s32[]{:S(2)}) async-start(), calls=%async_computation.4 | async-start | bytes 4718592 | tf_op jit(solution)/shard_map/all_gather | solution.py:11
  206.7 2.1 copy-start.3
  239.8 9.0 %copy-start.10 = (f32[16]{0:T(128)S(1)}, f32[16]{0:T(128)}, u32[]{:S(2)}) copy-start(f32[16]{0:T(128)} %param.27) | copy-start | bytes 196
  248.3 1.2 copy-start.4
  248.3 1.5 copy-start.7
Sparse Core Ops, SparseCore 0:
  49.0 86.2 all-reduce.1
Sparse Core Ops, SparseCore 1:
  52.0 27.9 all-gather.12
  81.8 54.2 all-gather.10
  152.9 35.9 all-gather.14
  198.5 36.5 all-gather.16
where the time goes:
time: 262 us; the launch traced here: 260 us
  waiting for transfers between devices  118 us (45%)
  blocking collectives  49.1 us (19%)
  other arithmetic  26.1 us (10%)
  matrix products  25.4 us (10%)
  local copies, waits for them, and re-layouts  24.4 us (9%)
  between operations  16.1 us (6%)
    psum x1, waiting for transfers between devices, body(): lax.psum(head_part.astype(jnp.bfloat16), 'tp').astype(jnp.float32)  75.9 us
    all_gather x2, waiting for transfers between devices, prefix(): pieces = jax.tree.map(lambda part: lax.all_gather(part, axis), value)  41.9 us
    all_gather x2, blocking collectives, prefix(): pieces = jax.tree.map(lambda part: lax.all_gather(part, axis), value)  18.2 us
    select_n x21, other arithmetic, lap(): jnp.where(position < mine, new, old)  16.5 us
    all_gather x1, blocking collectives, body(): value_piece = lax.all_gather(values_mine, 'ctx', axis=0, tiled=True)  11.2 us
    all_gather x1, blocking collectives, body(): key_piece = lax.all_gather(keys_mine, 'ctx', axis=0, tiled=True)  11.2 us
    unnamed x35, local copies, waits for them, and re-layouts  10.7 us
    all_gather x1, blocking collectives, body(): lax.all_gather(dt_proj, 'ctx', axis=0, tiled=True)  8.44 us
  transfers between devices with their start and end apart: 5, of which 3 were waited for; matrix products, arithmetic and copies ran while one was open for 8% of the time, Pallas kernels for 0%

commit v1 on v0

v1 whole, which is shorter than its diff:
```python
import functools
import math

import jax
import jax.numpy as jnp
from jax import lax
from jax.experimental import pallas as pl
from jax.experimental.pallas import tpu as pltpu
from jax.sharding import PartitionSpec as P

MESH = pl.DeviceIdType.MESH
BF16 = jnp.bfloat16
F32 = jnp.float32
LANES = 128


class RingGather:
    def __init__(self, own, slot, n_ctx, halves, send, recv, local):
        self.slot, self.halves, self.own = slot, halves, own
        self.send, self.recv, self.local = send, recv, local
        me = lax.axis_index("ctx")
        self.me, self.core = me, me % 2
        chips = n_ctx // 2
        self.chips = chips
        self.steps = chips // 2
        self.width = math.isqrt(chips)
        chip = me // 2
        row = chip // self.width
        col = chip % self.width
        self.place = row * self.width + col + (row % 2) * (self.width - 1 - 2 * col)
        self.right = self.chip_at(1) * 2 + self.core
        self.left = self.chip_at(chips - 1) * 2 + self.core
        self.partner = (me // 2) * 2 + 1 - self.core
        self.sent = []

    def chip_at(self, ahead):
        place = (self.place + ahead) % self.chips
        row = place // self.width
        col = place % self.width
        return row * self.width + col + (row % 2) * (self.width - 1 - 2 * col)

    def neighbours(self):
        return [self.right, self.left, self.partner]

    def part(self, step, way):
        return None if step < self.steps else way

    def copy(self, src, dst, sem, to):
        return pltpu.make_async_remote_copy(
            src_ref=src,
            dst_ref=dst,
            send_sem=self.send.at[sem],
            recv_sem=self.recv.at[sem],
            device_id={"ctx": to},
            device_id_type=MESH,
        )

    def ring_sem(self, step, way):
        return 2 * (step - 1) + way

    def pair_sem(self, step, way):
        return 2 * self.steps + 1 + 2 * (step - 1) + way

    def start(self):
        self.keep = pltpu.make_async_copy(self.own, self.slot(self.me, None), self.local)
        self.keep.start()
        for way, to in ((0, self.right), (1, self.left)):
            part = self.part(1, way)
            src = self.own if part is None else self.halves(part)
            self.go(self.copy(src, self.slot(self.me, part), self.ring_sem(1, way), to))
        self.go(self.copy(self.own, self.slot(self.me, None), 2 * self.steps, self.partner))

    def go(self, copy):
        copy.start()
        self.sent.append(copy)

    def step(self, step):
        for way, to in ((0, self.right), (1, self.left)):
            ahead = self.chips - step if way == 0 else step
            shard = self.chip_at(ahead) * 2 + self.core
            place = self.slot(shard, self.part(step, way))
            self.copy(place, place, self.ring_sem(step, way), to).wait_recv()
            if step < self.steps:
                passed = self.slot(shard, self.part(step + 1, way))
                self.go(self.copy(passed, passed, self.ring_sem(step + 1, way), to))
            self.go(self.copy(place, place, self.pair_sem(step, way), self.partner))

    def finish(self):
        self.keep.wait()
        other = 1 - self.core
        place = self.slot(self.chip_at(0) * 2 + other, None)
        self.copy(place, place, 2 * self.steps, self.partner).wait_recv()
        for step in range(1, self.steps + 1):
            for way in (0, 1):
                ahead = self.chips - step if way == 0 else step
                shard = self.chip_at(ahead) * 2 + other
                place = self.slot(shard, self.part(step, way))
                self.copy(place, place, self.pair_sem(step, way), self.partner).wait_recv()

    def drain(self):
        for copy in self.sent:
            copy.wait_send()


class LineGather:
    def __init__(self, buffer, n_tp, send, recv):
        self.buffer, self.n_tp, self.send, self.recv = buffer, n_tp, send, recv
        self.me = lax.axis_index("tp")

    def copy(self, index, step, way, to):
        return pltpu.make_async_remote_copy(
            src_ref=self.buffer.at[index],
            dst_ref=self.buffer.at[index],
            send_sem=self.send.at[2 * (step - 1) + way],
            recv_sem=self.recv.at[2 * (step - 1) + way],
            device_id={"tp": to},
            device_id_type=MESH,
        )

    def launch(self, step):
        me = self.me

        @pl.when((me + 1 < self.n_tp) & (me - step + 1 >= 0))
        def _():
            self.copy(me - step + 1, step, 0, me + 1).start()

        @pl.when((me >= 1) & (me + step - 1 < self.n_tp))
        def _():
            self.copy(me + step - 1, step, 1, me - 1).start()

    def run(self, use):
        me = self.me
        for step in range(1, self.n_tp):

            @pl.when(me - step >= 0)
            def _():
                self.copy(me - step, step, 0, me).wait_recv()

            @pl.when(me + step < self.n_tp)
            def _():
                self.copy(me + step, step, 1, me).wait_recv()

            if step + 1 < self.n_tp:
                self.launch(step + 1)

            @pl.when(me - step >= 0)
            def _():
                use(me - step)

            @pl.when(me + step < self.n_tp)
            def _():
                use(me + step)

    def drain(self):
        me = self.me
        for step in range(1, self.n_tp):

            @pl.when((me + 1 < self.n_tp) & (me - step + 1 >= 0))
            def _():
                self.copy(me - step + 1, step, 0, me).wait_send()

            @pl.when((me >= 1) & (me + step - 1 < self.n_tp))
            def _():
                self.copy(me + step - 1, step, 1, me).wait_send()


def barrier_with(devices):
    barrier = pltpu.get_barrier_semaphore()
    for device in devices:
        pl.semaphore_signal(barrier, inc=1, device_id=device, device_id_type=MESH)
    pl.semaphore_wait(barrier, len(devices))


def front_kernel(
    n_ctx,
    n_tp,
    heads,
    widths,
    q_ref,
    kv_ref,
    hidden_ref,
    out_ref,
    gain_ref,
    w_ref,
    res_ref,
    x_ref,
    bc_ref,
    dt_ref,
    kv_all,
    w_all,
    o_all,
    o_full,
    att_all,
    res_all,
    hidden_mine,
    q_rows,
    scores,
    top,
    total,
    mixed,
    sums,
    proj,
    square,
    kv_send,
    kv_recv,
    o_send,
    o_recv,
    w_send,
    w_recv,
    t_send,
    t_recv,
    a_send,
    a_recv,
    r_send,
    r_recv,
    local,
):
    ctx = lax.axis_index("ctx")
    tp = lax.axis_index("tp")
    tok = q_ref.shape[0]
    half = tok // 2
    head_dim = kv_ref.shape[1] // 2
    cols = hidden_mine.shape[1]
    depth = w_ref.shape[0]
    slab = out_ref.shape[0]
    piece = o_all.shape[1] // n_ctx
    repeat = piece * n_ctx // slab

    def kv_slot(i, part):
        if part is None:
            return kv_all.at[pl.ds(pl.multiple_of(i * tok, tok), tok)]
        return kv_all.at[pl.ds(pl.multiple_of(i * tok + part * half, half), half)]

    def w_slot(i, part):
        if part is None:
            return w_all.at[pl.ds(pl.multiple_of(i * depth, depth), depth)]
        return w_all.at[pl.ds(pl.multiple_of(i * depth + part * (depth // 2), depth // 2), depth // 2)]

    def o_slot(i, part):
        rows = pl.ds(pl.multiple_of(i * piece, piece), piece)
        if part is None:
            return o_all.at[:, rows]
        return o_all.at[pl.ds(part * (n_tp // 2), n_tp // 2), rows]

    kv = RingGather(
        kv_ref, kv_slot, n_ctx, lambda part: kv_ref.at[pl.ds(part * half, half)],
        kv_send, kv_recv, local.at[0],
    )
    w = RingGather(
        w_ref, w_slot, n_ctx, lambda part: w_ref.at[pl.ds(part * (depth // 2), depth // 2)],
        w_send, w_recv, local.at[1],
    )
    o = RingGather(
        o_slot(ctx, None), o_slot, n_ctx, lambda part: o_slot(ctx, part),
        o_send, o_recv, local.at[2],
    )
    barrier_with(
        [{"ctx": to} for to in kv.neighbours()]
        + [{"tp": (tp + ahead) % n_tp} for ahead in range(1, n_tp)]
    )

    kv.start()
    my_rows = pl.ds(pl.multiple_of((ctx // repeat) * piece, piece), piece)
    my_place = pl.ds(pl.multiple_of(ctx * piece, piece), piece)

    def o_columns(t):
        return out_ref.at[my_rows, pl.ds(pl.multiple_of(t * cols, cols), cols)]

    swaps = []
    for ahead in range(1, n_tp):
        to = (tp + ahead) % n_tp
        swap = pltpu.make_async_remote_copy(
            src_ref=o_columns(to),
            dst_ref=o_all.at[tp, my_place],
            send_sem=t_send.at[ahead],
            recv_sem=t_recv.at[ahead],
            device_id={"tp": to},
            device_id_type=MESH,
        )
        swap.start()
        swaps.append(swap)
    keep_o = pltpu.make_async_copy(o_columns(tp), o_all.at[tp, my_place], local.at[3])
    keep_o.start()
    get_hidden = pltpu.make_async_copy(
        hidden_ref.at[:, pl.ds(pl.multiple_of(tp * cols, cols), cols)], hidden_mine, local.at[4]
    )
    get_hidden.start()

    for part in range(2):
        for head in range(heads):
            q_rows[part, head * half : (head + 1) * half, :] = q_ref[
                part * half : (part + 1) * half, head * head_dim : (head + 1) * head_dim
            ]
    top[...] = jnp.full_like(top, -1e30)
    total[...] = jnp.zeros_like(total)
    mixed[...] = jnp.zeros_like(mixed)

    for step in range(1, kv.steps + 1):
        kv.step(step)

    for ahead, swap in zip(range(1, n_tp), swaps):
        swap.wait_recv()
    keep_o.wait()
    for way, to in ((0, o.right), (1, o.left)):
        place = o_slot(ctx, o.part(1, way))
        o.go(o.copy(place, place, o.ring_sem(1, way), to))
    place = o_slot(ctx, None)
    o.go(o.copy(place, place, 2 * o.steps, o.partner))
    kv.finish()

    scale = 1.0 / math.sqrt(head_dim)
    rows = heads * half
    row_at = lax.broadcasted_iota(jnp.int32, (rows, half), 0) % half
    col_at = lax.broadcasted_iota(jnp.int32, (rows, half), 1)
    causal = col_at <= row_at

    def place_of(unit):
        late = (unit - ctx - 1 + n_ctx) // n_ctx
        shard = unit - late
        return late, shard, shard * tok + late * half

    def block_scores(part, start):
        keys = kv_all[pl.ds(pl.multiple_of(start, half), half), :head_dim]
        return lax.dot_general(
            q_rows[part], keys, (((1,), (1,)), ((), ())), preferred_element_type=F32
        ) * scale

    def early_scores(j, carry):
        found = block_scores(1, j * tok)
        scores[j] = found
        top[1] = jnp.maximum(top[1], found)
        return carry

    def mixed_scores(unit, carry):
        late, shard, start = place_of(unit)
        found = block_scores(late, start)
        found = jnp.where(causal | (shard != ctx), found, -1e30)
        scores[n_ctx + unit] = found
        top[late] = jnp.maximum(top[late], found)
        return carry

    lax.fori_loop(0, n_ctx, early_scores, 0)
    lax.fori_loop(0, n_ctx + 1, mixed_scores, 0)
    o.step(1)
    for part in range(2):
        top[part] = jnp.broadcast_to(jnp.max(top[part], axis=1, keepdims=True), (rows, half))

    def add_block(slot, part, start):
        weights = jnp.exp(scores[slot] - top[part])
        total[part] = total[part] + weights
        values = kv_all[pl.ds(pl.multiple_of(start, half), half), head_dim:]
        mixed[part] = mixed[part] + jnp.dot(weights.astype(BF16), values, preferred_element_type=F32)

    def early_values(j, carry):
        add_block(j, 1, j * tok)
        return carry

    def mixed_values(unit, carry):
        late, shard, start = place_of(unit)
        add_block(n_ctx + unit, late, start)
        return carry

    lax.fori_loop(0, n_ctx, early_values, 0)
    lax.fori_loop(0, n_ctx + 1, mixed_values, 0)
    for part in range(2):
        ended = (mixed[part] / jnp.sum(total[part], axis=1, keepdims=True)).astype(BF16)
        for head in range(heads):
            att_all[
                tp, part * half : (part + 1) * half, head * head_dim : (head + 1) * head_dim
            ] = ended[head * half : (head + 1) * half]

    attended = LineGather(att_all, n_tp, a_send, a_recv)
    attended.launch(1)
    for step in range(2, o.steps + 1):
        o.step(step)
    w.start()
    get_hidden.wait()
    other = 1 - o.core
    place = o_slot(o.chip_at(0) * 2 + other, None)
    o.copy(place, place, 2 * o.steps, o.partner).wait_recv()
    for step in range(1, o.steps + 1):
        for way in (0, 1):
            ahead = o.chips - step if way == 0 else step
            place = o_slot(o.chip_at(ahead) * 2 + other, o.part(step, way))
            o.copy(place, place, o.pair_sem(step, way), o.partner).wait_recv()
    if repeat > 1:
        for i in range(slab // piece):
            o_full[:, i * piece : (i + 1) * piece] = o_all[:, i * repeat * piece : (i * repeat + 1) * piece]
    weight = o_full if repeat > 1 else o_all

    sums[...] = jnp.zeros_like(sums)

    def add_heads(t):
        part = jnp.dot(att_all[t], weight[t], preferred_element_type=F32)
        sums[...] += part.astype(BF16).astype(F32)

    add_heads(tp)
    attended.run(add_heads)
    mine = (hidden_mine[...].astype(F32) + sums[...]).astype(BF16)
    res_ref[...] = mine
    res_all[tp] = mine
    residual = LineGather(res_all, n_tp, r_send, r_recv)
    residual.launch(1)

    for step in range(1, w.steps + 1):
        w.step(step)
    w.finish()
    proj[...] = jnp.zeros_like(proj)
    square[...] = jnp.zeros_like(square)

    def add_features(t):
        part = res_all[t].astype(F32)
        squares = part * part
        folded = squares[:, :LANES]
        for i in range(1, cols // LANES):
            folded = folded + squares[:, i * LANES : (i + 1) * LANES]
        square[...] += folded
        scaled = (part * gain_ref[t]).astype(BF16)
        proj[...] += jnp.dot(
            scaled,
            w_all[pl.ds(pl.multiple_of(t * cols, cols), cols), :],
            preferred_element_type=F32,
        )

    add_features(tp)
    residual.run(add_features)
    mean = jnp.sum(square[...], axis=1, keepdims=True) / (cols * n_tp)
    inverse = lax.rsqrt(mean + 1e-05)
    x_wide, bc_wide = widths
    x_ref[...] = (proj[:, :x_wide] * inverse).astype(BF16)
    bc_ref[...] = (proj[:, x_wide : x_wide + bc_wide] * inverse).astype(BF16)
    dt_ref[...] = proj[:, x_wide + bc_wide :] * inverse

    kv.drain()
    o.drain()
    w.drain()
    for swap in swaps:
        swap.wait_send()
    attended.drain()
    residual.drain()


def front(n_ctx, n_tp, queries, kv, hidden, out_proj, gain, weights, widths):
    tok, q_wide = queries.shape
    head_dim = kv.shape[1] // 2
    heads = q_wide // head_dim
    half = tok // 2
    cols = hidden.shape[1] // n_tp
    slab = out_proj.shape[0]
    piece = max(16, slab // n_ctx)
    repeat = piece * n_ctx // slab
    rows = heads * half
    ring = 4 * (n_ctx // 4) + 1
    line = 2 * (n_tp - 1)
    vmem = pl.BlockSpec(memory_space=pltpu.VMEM)
    hbm = pl.BlockSpec(memory_space=pl.ANY)
    wide = weights.shape[1]
    dma = pltpu.SemaphoreType.DMA
    return pl.pallas_call(
        functools.partial(front_kernel, n_ctx, n_tp, heads, widths),
        out_shape=(
            jax.ShapeDtypeStruct((tok, cols), BF16),
            jax.ShapeDtypeStruct((tok, widths[0]), BF16),
            jax.ShapeDtypeStruct((tok, widths[1]), BF16),
            jax.ShapeDtypeStruct((tok, wide - widths[0] - widths[1]), F32),
        ),
        in_specs=[vmem, vmem, hbm, hbm, vmem, hbm],
        out_specs=(vmem,) * 4,
        scratch_shapes=[
            pltpu.VMEM((n_ctx * tok, 2 * head_dim), BF16),
            pltpu.VMEM((n_ctx * weights.shape[0], wide), BF16),
            pltpu.VMEM((n_tp, n_ctx * piece, cols), BF16),
            pltpu.VMEM((n_tp, slab, cols) if repeat > 1 else (1, 16, LANES), BF16),
            pltpu.VMEM((n_tp, tok, q_wide), BF16),
            pltpu.VMEM((n_tp, tok, cols), BF16),
            pltpu.VMEM((tok, cols), BF16),
            pltpu.VMEM((2, rows, head_dim), BF16),
            pltpu.VMEM((2 * n_ctx + 1, rows, half), F32),
            pltpu.VMEM((2, rows, half), F32),
            pltpu.VMEM((2, rows, half), F32),
            pltpu.VMEM((2, rows, head_dim), F32),
            pltpu.VMEM((tok, cols), F32),
            pltpu.VMEM((tok, wide), F32),
            pltpu.VMEM((tok, LANES), F32),
            dma((ring,)),
            dma((ring,)),
            dma((ring,)),
            dma((ring,)),
            dma((ring,)),
            dma((ring,)),
            dma((n_tp,)),
            dma((n_tp,)),
            dma((line,)),
            dma((line,)),
            dma((line,)),
            dma((line,)),
            dma((5,)),
        ],
        compiler_params=pltpu.CompilerParams(
            collective_id=0, has_side_effects=True, vmem_limit_bytes=56 * 1024 * 1024
        ),
    )(queries, kv, hidden, out_proj, gain.reshape(n_tp, 1, cols), weights)


def exact_dot(a, b, dims):
    return lax.dot_general(
        a, b, (dims, ((), ())), precision=lax.Precision.HIGHEST, preferred_element_type=F32
    )


def mixer_kernel(
    n_ctx,
    m_local,
    x_ref,
    bc_ref,
    dt_ref,
    bias_ref,
    log_ref,
    skip_ref,
    y_ref,
    state_out,
    state_in,
    log_out,
    log_in,
    enter_out,
    enter_in,
    rows_in,
    grown,
    inner,
    s_send,
    s_recv,
    l_send,
    l_recv,
    e_send,
    e_recv,
):
    me = lax.axis_index("ctx")
    tok, wide = x_ref.shape
    half = tok // 2
    state = bc_ref.shape[1] // 2
    head_wide = wide // m_local
    share = wide // n_ctx
    barrier_with([{"ctx": (me + ahead) % n_ctx} for ahead in range(1, n_ctx)])

    spread = (
        lax.broadcasted_iota(jnp.int32, (LANES, wide), 1) // head_wide
        == lax.broadcasted_iota(jnp.int32, (LANES, wide), 0)
    ).astype(F32)
    across = lax.broadcasted_iota(jnp.int32, (half, half), 1)
    down = lax.broadcasted_iota(jnp.int32, (half, half), 0)
    causal = across <= down
    lower = causal.astype(F32)
    rates = -jnp.exp(log_ref[...])
    kept = []
    log_out[...] = jnp.zeros_like(log_out)
    for chunk in range(2):
        at = slice(chunk * half, (chunk + 1) * half)
        steps = jax.nn.softplus(dt_ref[at, :] + bias_ref[...])
        cumul = exact_dot(lower, steps * rates, ((1,), (0,)))
        last = cumul[half - 1 : half, :]
        log_out[chunk : chunk + 1, :] = last
        tail = exact_dot(jnp.exp(last - cumul) * steps, spread, ((1,), (0,)))
        weighted = (x_ref[at, :].astype(F32) * tail).astype(BF16)
        made = lax.dot_general(
            weighted, bc_ref[at, :state], (((0,), (0,)), ((), ())), preferred_element_type=F32
        ).astype(BF16)
        for i in range(n_ctx):
            state_out[i, chunk * share : (chunk + 1) * share, :] = made[i * share : (i + 1) * share]
        grown[at, :] = exact_dot(jnp.exp(cumul), spread, ((1,), (0,)))
        kept.append((cumul, steps))

    def transfer(src, dst, send, recv, ahead):
        return pltpu.make_async_remote_copy(
            src_ref=src,
            dst_ref=dst,
            send_sem=send.at[ahead],
            recv_sem=recv.at[ahead],
            device_id={"ctx": (me + ahead) % n_ctx},
            device_id_type=MESH,
        )

    copies = []
    for ahead in range(1, n_ctx):
        to = (me + ahead) % n_ctx
        for copy in (
            transfer(state_out.at[to], state_in.at[me], s_send, s_recv, ahead),
            transfer(log_out, log_in.at[me], l_send, l_recv, ahead),
        ):
            copy.start()
            copies.append(copy)
    state_in[me] = state_out[me]
    log_in[me] = log_out[...]

    for chunk in range(2):
        at = slice(chunk * half, (chunk + 1) * half)
        cumul, steps = kept[chunk]
        cumul_t, steps_t = cumul.T, steps.T
        gram = lax.dot_general(
            bc_ref[at, state:], bc_ref[at, :state], (((1,), (1,)), ((), ())),
            preferred_element_type=F32,
        )
        gram = jnp.where(causal, gram, 0.0)
        per = LANES // head_wide
        for pair in range(m_local // per):
            lanes = slice(pair * LANES, (pair + 1) * LANES)
            x_pair = x_ref[at, lanes]
            found = None
            for k in range(per):
                head = pair * per + k
                gap = jnp.where(causal, cumul[:, head : head + 1] - cumul_t[head : head + 1, :], 0.0)
                mixing = gram * jnp.exp(gap) * steps_t[head : head + 1, :]
                one = jnp.dot(mixing.astype(BF16), x_pair, preferred_element_type=F32)
                found = one if k == 0 else jnp.where(across // head_wide == k, one, found)
            inner[at, lanes] = found + skip_ref[:, lanes] * x_pair.astype(F32)

    for ahead in range(1, n_ctx):
        src = (me + n_ctx - ahead) % n_ctx
        transfer(state_out.at[src], state_in.at[src], s_send, s_recv, ahead).wait_recv()
        transfer(log_out, log_in.at[src], l_send, l_recv, ahead).wait_recv()

    chosen = (
        (me * share + lax.broadcasted_iota(jnp.int32, (share, LANES), 0)) // head_wide
        == lax.broadcasted_iota(jnp.int32, (share, LANES), 1)
    ).astype(F32)
    running = jnp.zeros((share, state), F32)
    for block in range(2 * n_ctx):
        chunk = block // n_ctx
        src = block if chunk == 0 else 2 * n_ctx - 1 - block
        rows = slice(chunk * share, (chunk + 1) * share)
        enter_out[src, rows, :] = running.astype(BF16)
        logs = jnp.sum(chosen * log_in[src, chunk : chunk + 1, :], axis=1, keepdims=True)
        running = jnp.exp(logs) * running + state_in[src, rows, :].astype(F32)

    for ahead in range(1, n_ctx):
        to = (me + ahead) % n_ctx
        copy = transfer(enter_out.at[to], enter_in.at[me], e_send, e_recv, ahead)
        copy.start()
        copies.append(copy)
    enter_in[me] = enter_out[me]
    for ahead in range(1, n_ctx):
        src = (me + n_ctx - ahead) % n_ctx
        transfer(enter_out.at[src], enter_in.at[src], e_send, e_recv, ahead).wait_recv()
    for chunk in range(2):
        at = slice(chunk * half, (chunk + 1) * half)
        for i in range(n_ctx):
            rows_in[i * share : (i + 1) * share, :] = enter_in[
                i, chunk * share : (chunk + 1) * share, :
            ].astype(F32)
        carried = lax.dot_general(
            bc_ref[at, state:], rows_in[...].astype(BF16), (((1,), (1,)), ((), ())),
            preferred_element_type=F32,
        )
        y_ref[at, :] = (inner[at, :] + grown[at, :] * carried).astype(BF16)
    for copy in copies:
        copy.wait_send()


def mixer(n_ctx, m_local, x, bc, dt, bias, logs, skip):
    tok, wide = x.shape
    state = bc.shape[1] // 2
    share = wide // n_ctx
    vmem = pl.BlockSpec(memory_space=pltpu.VMEM)
    dma = pltpu.SemaphoreType.DMA
    return pl.pallas_call(
        functools.partial(mixer_kernel, n_ctx, m_local),
        out_shape=jax.ShapeDtypeStruct((tok, wide), BF16),
        in_specs=[vmem] * 6,
        out_specs=vmem,
        scratch_shapes=[
            pltpu.VMEM((n_ctx, 2 * share, state), BF16),
            pltpu.VMEM((n_ctx, 2 * share, state), BF16),
            pltpu.VMEM((8, LANES), F32),
            pltpu.VMEM((n_ctx, 8, LANES), F32),
            pltpu.VMEM((n_ctx, 2 * share, state), BF16),
            pltpu.VMEM((n_ctx, 2 * share, state), BF16),
            pltpu.VMEM((wide, state), F32),
            pltpu.VMEM((tok, wide), F32),
            pltpu.VMEM((tok, wide), F32),
        ]
        + [dma((n_ctx,))] * 6,
        compiler_params=pltpu.CompilerParams(
            collective_id=1, has_side_effects=True, vmem_limit_bytes=32 * 1024 * 1024
        ),
    )(x, bc, dt, bias, logs, skip)


def body(
    queries,
    key_heads,
    head_values,
    hidden,
    out_proj,
    norm_gain,
    x_proj,
    bc_proj,
    dt_proj,
    dt_bias,
    decay_log,
    skip_gain,
):
    n_ctx = lax.axis_size("ctx")
    n_tp = lax.axis_size("tp")
    tp = lax.axis_index("tp")
    head_dim = key_heads.shape[2]
    q_local = queries.shape[1] // head_dim
    group = q_local * n_tp // key_heads.shape[1]
    m_local = skip_gain.shape[0]
    per_group = m_local * n_tp // bc_proj.shape[1]
    assert q_local <= group and m_local <= per_group
    kv_head = tp * q_local // group
    kv = jnp.concatenate(
        [
            lax.dynamic_index_in_dim(key_heads, kv_head, 1, False),
            lax.dynamic_index_in_dim(head_values, kv_head, 1, False),
        ],
        axis=1,
    )
    bc_mine = lax.dynamic_index_in_dim(bc_proj, tp * m_local // per_group, 1, False)
    pad = LANES - m_local
    weights = jnp.concatenate([x_proj, bc_mine, jnp.pad(dt_proj, ((0, 0), (0, pad)))], axis=1)
    widths = (x_proj.shape[1], bc_mine.shape[1])
    residual_out, x, bc, dt = front(
        n_ctx, n_tp, queries, kv, hidden, out_proj, norm_gain, weights, widths
    )
    bias = jnp.pad(dt_bias, (0, pad)).reshape(1, LANES)
    logs = jnp.pad(decay_log, (0, pad)).reshape(1, LANES)
    skip = jnp.repeat(skip_gain, x_proj.shape[1] // m_local).reshape(1, -1)
    mamba_out = mixer(n_ctx, m_local, x, bc, dt, bias, logs, skip)
    return (residual_out, mamba_out)


def solution(mesh):
    placed = (
        P("ctx", "tp"),
        P("ctx", None, None),
        P("ctx", None, None),
        P("ctx", None),
        P("tp", None),
        P(),
        P("ctx", "tp"),
        P("ctx", None, None),
        P("ctx", "tp"),
        P("tp"),
        P("tp"),
        P("tp"),
    )
    return jax.shard_map(
        body,
        mesh=mesh,
        in_specs=placed,
        out_specs=(P("ctx", "tp"), P("ctx", "tp")),
        check_vma=False,
    )
```

time: 262 us -> 146 us (0.56)
  Pallas kernels: 0 us -> 133 us
  waiting for transfers between devices: 118 us -> 0 us
  blocking collectives: 49.1 us -> 0 us
  matrix products: 25.4 us -> 0 us
  other arithmetic: 26.1 us -> 3.14 us
  local copies, waits for them, and re-layouts: 24.4 us -> 8.59 us
  between operations: 16.1 us -> 0.76 us
    pallas_call x0 -> x2, Pallas kernels: none -> 133 us  [the longest x1 114 us: front(): pl.pallas_call(functools.partial(front_kernel, n_ctx, n_tp, heads, widths...]
    psum x1 -> x0, waiting for transfers between devices: 75.9 us -> none  [body(): lax.psum(head_part.astype(jnp.bfloat16), 'tp').astype(jnp.float32)]
    all_gather x5 -> x0, blocking collectives: 49.1 us -> none  [the longest x2 18.2 us: prefix(): pieces = jax.tree.map(lambda part: lax.all_gather(part, axis), value)]
    all_gather x4 -> x0, waiting for transfers between devices: 42 us -> none  [the longest x2 41.9 us: prefix(): pieces = jax.tree.map(lambda part: lax.all_gather(part, axis), value)]
    dot_general x13 -> x0, matrix products: 25.4 us -> none  [the longest x1 6.55 us: body(): jnp.dot(normed, lax.all_gather(x_proj, 'ctx', axis=0, tiled=True), prefer...]
    select_n x23 -> x0, other arithmetic: 17.6 us -> none  [the longest x21 16.5 us: lap(): jnp.where(position < mine, new, old)]
    reduce_sum x2 -> x0, other arithmetic: 7.67 us -> none  [the longest x1 4.5 us: body(): run_sum = jnp.sum(weights, axis=-1)]
    convert_element_type x2 -> x0, local copies, waits for them, and re-layouts: 6.17 us -> none  [body(): inputs = inputs_low.astype(jnp.float32)]
  transfers between devices with their start and end apart: 5 -> 0, of which waited for: 3 -> 0; matrix products, arithmetic and copies ran while one was open for 8% -> 0% of each run, Pallas kernels for 0% -> 0%
where the time goes in v1:
time: 146 us
  Pallas kernels  133 us (91%)
  local copies, waits for them, and re-layouts  8.59 us (6%)
  other arithmetic  3.14 us (2%)
    pallas_call x1, Pallas kernels, front(): pl.pallas_call(functools.partial(front_kernel, n_ctx, n_tp, heads, widths...  114 us
    pallas_call x1, Pallas kernels, mixer(): pl.pallas_call(functools.partial(mixer_kernel, n_ctx, m_local), out_shape...  19.8 us
    unnamed x24, local copies, waits for them, and re-layouts  7.62 us

profile of v1, /device:TPU:1, one launch (start us, length us, event | category | flops | bytes accessed | tf_op | source)
XLA Modules:
  0.0 145.8 jit_solution(14958923598999300645)
XLA Ops:
  0.6 0.0 copy-start
  0.6 0.0 copy-start.5
  0.7 0.0 copy-start.4
  0.7 1.2 copy-done
  1.9 0.5 constant_dynamic-slice_fusion
  2.5 0.8 copy.18
  3.3 2.5 %fusion.1.w_ref = bf16[512,1408]{1,0:T(8,128)(2,1)} fusion(bf16[512,16]{1,0:T(8,128)(2,1)S(1)} %copy.18, bf16[512,256]{1,0:T(8,128)(2,1)S(1)} %bitcast.14, bf16[512,1024]{1,0:T(8,128)(2,1)} %param.18), kind=kLoop, calls=%fused_computation.2 | loop fusion | flops 5767168 | bytes 2768896 | tf_op jit(solution)/shard_map/concatenate | solution.py:720
  5.8 0.0 copy-done.5
  5.8 0.0 copy-done.4
  5.8 0.3 constant_dynamic-slice_fusion.1
  6.1 0.7 pad_maximum_fusion.kv_ref
  6.8 0.0 copy-start.7
  6.8 0.0 copy-start.8
  6.8 0.0 copy-start.6
  6.8 113.5 %shard_map.131 = (bf16[256,1024]{1,0:T(8,128)(2,1)}, bf16[256,1024]{1,0:T(8,128)(2,1)}, bf16[256,256]{1,0:T(8,128)(2,1)}, f32[256,128]{1,0:T(8,128)}) custom-call(bf16[256,512]{1,0:T(8,128)(2,1)} %q_ref.1, bf16[256,256]{1,0:T(8,128)(2,1)} %pad_maximum_fusion.kv_ref, bf16[256,4096]{1,0:T(8,128)(2,1)} %hidden_ref.1, bf16[512,4096]{1,0:T(8,128)(2,1)} %out_ref.1, ...), custom_call_target="tpu_custom_call" | custom-call | tf_op jit(solution)/shard_map/pallas_call | solution.py:459
  120.3 0.0 copy-done.7
  120.3 0.0 copy-done.8
  120.3 0.0 copy-done.6
  120.3 0.1 broadcast_in_dim.3
  120.4 0.1 reshape_reshape.3.skip_ref
  120.5 0.0 copy-start.1
  120.5 1.0 copy-done.1
  121.5 0.0 copy-start.2
  121.5 0.9 copy-done.2
  122.4 0.0 copy-start.3
  122.4 0.9 copy-done.3
  123.3 19.8 %shard_map.132 = bf16[256,1024]{1,0:T(8,128)(2,1)S(1)} custom-call(bf16[256,1024]{1,0:T(8,128)(2,1)S(1)} %copy-done.1, bf16[256,256]{1,0:T(8,128)(2,1)S(1)} %copy-done.2, f32[256,128]{1,0:T(8,128)S(1)} %copy-done.3, f32[1,128]{1,0:T(1,128)S(1)} %get-tuple-element.13.bias_ref, f32[1,128]{1,0:T(1,128)S(1)} %get-tuple-element.12.log_ref, ...), custom_call_target="tpu_custom_call" | custom-call | tf_op jit(solution)/shard_map/pallas_call | solution.py:664
  143.1 1.9 %copy.30 = bf16[256,1024]{1,0:T(8,128)(2,1)} copy(bf16[256,1024]{1,0:T(8,128)(2,1)} %get-tuple-element.16) | data formatting | bytes 1048576
  145.0 0.8 copy.31
  (4 shorter events, 0.1 us)
Async XLA Ops:
  0.6 1.2 copy-start
  0.6 5.1 %copy-start.5 = (bf16[256,4,128]{2,1,0:T(4,128)(2,1)S(1)}, bf16[256,4,128]{2,1,0:T(4,128)(2,1)}, u32[]{:S(2)}) copy-start(bf16[256,4,128]{2,1,0:T(4,128)(2,1)} %param.13) | copy-start | bytes 786436
  0.7 5.1 %copy-start.4 = (bf16[256,4,128]{2,1,0:T(4,128)(2,1)S(1)}, bf16[256,4,128]{2,1,0:T(4,128)(2,1)}, u32[]{:S(2)}) copy-start(bf16[256,4,128]{2,1,0:T(4,128)(2,1)} %param.14) | copy-start | bytes 786436
  6.8 113.5 %copy-start.7 = (f32[16]{0:T(128)S(1)}, f32[16]{0:T(128)}, u32[]{:S(2)}) copy-start(f32[16]{0:T(128)} %param.22) | copy-start | bytes 196
  6.8 113.5 %copy-start.8 = (f32[16]{0:T(128)S(1)}, f32[16]{0:T(128)}, u32[]{:S(2)}) copy-start(f32[16]{0:T(128)} %param.21) | copy-start | bytes 196
  6.8 113.6 %copy-start.6 = (f32[16]{0:T(128)S(1)}, f32[16]{0:T(128)}, u32[]{:S(2)}) copy-start(f32[16]{0:T(128)} %param.23) | copy-start | bytes 196
  120.5 1.0 copy-start.1
  121.5 0.9 copy-start.2
  122.4 0.9 copy-start.3

commit v2 on v1

--- a/solution.py
+++ b/solution.py
@@ -62,8 +62,9 @@
         return 2 * self.steps + 1 + 2 * (step - 1) + way
 
     def start(self):
-        self.keep = pltpu.make_async_copy(self.own, self.slot(self.me, None), self.local)
-        self.keep.start()
+        if self.local is not None:
+            self.keep = pltpu.make_async_copy(self.own, self.slot(self.me, None), self.local)
+            self.keep.start()
         for way, to in ((0, self.right), (1, self.left)):
             part = self.part(1, way)
             src = self.own if part is None else self.halves(part)
@@ -86,7 +87,8 @@
             self.go(self.copy(place, place, self.pair_sem(step, way), self.partner))
 
     def finish(self):
-        self.keep.wait()
+        if self.local is not None:
+            self.keep.wait()
         other = 1 - self.core
         place = self.slot(self.chip_at(0) * 2 + other, None)
         self.copy(place, place, 2 * self.steps, self.partner).wait_recv()
@@ -128,28 +130,30 @@
         def _():
             self.copy(me + step - 1, step, 1, me - 1).start()
 
-    def run(self, use):
+    def arrive(self, step):
         me = self.me
-        for step in range(1, self.n_tp):
-
-            @pl.when(me - step >= 0)
-            def _():
-                self.copy(me - step, step, 0, me).wait_recv()
-
-            @pl.when(me + step < self.n_tp)
-            def _():
-                self.copy(me + step, step, 1, me).wait_recv()
-
-            if step + 1 < self.n_tp:
-                self.launch(step + 1)
-
-            @pl.when(me - step >= 0)
-            def _():
-                use(me - step)
-
-            @pl.when(me + step < self.n_tp)
-            def _():
-                use(me + step)
+
+        @pl.when(me - step >= 0)
+        def _():
+            self.copy(me - step, step, 0, me).wait_recv()
+
+        @pl.when(me + step < self.n_tp)
+        def _():
+            self.copy(me + step, step, 1, me).wait_recv()
+
+        if step + 1 < self.n_tp:
+            self.launch(step + 1)
+
+    def use(self, step, take):
+        me = self.me
+
+        @pl.when(me - step >= 0)
+        def _():
+            take(me - step)
+
+        @pl.when(me + step < self.n_tp)
+        def _():
+            take(me + step)
 
     def drain(self):
         me = self.me
@@ -171,23 +175,31 @@
     pl.semaphore_wait(barrier, len(devices))
 
 
-def front_kernel(
+CHUNKS = 4
+
+
+def whole_kernel(
     n_ctx,
     n_tp,
     heads,
-    widths,
+    m_local,
     q_ref,
     kv_ref,
     hidden_ref,
     out_ref,
     gain_ref,
-    w_ref,
+    x_proj_ref,
+    bc_proj_ref,
+    dt_proj_ref,
+    bias_ref,
+    log_ref,
+    skip_ref,
     res_ref,
-    x_ref,
-    bc_ref,
-    dt_ref,
+    y_ref,
     kv_all,
-    w_all,
+    x_all,
+    bc_all,
+    dt_all,
     o_all,
     o_full,
     att_all,
@@ -199,16 +211,19 @@
     total,
     mixed,
     sums,
-    proj,
+    x_sum,
+    bc_sum,
+    dt_sum,
     square,
-    kv_send,
-    kv_recv,
-    o_send,
-    o_recv,
-    w_send,
-    w_recv,
+    x_low,
+    bc_low,
+    mixer_scratch,
+    ring_send,
+    ring_recv,
     t_send,
     t_recv,
+    d_send,
+    d_recv,
     a_send,
     a_recv,
     r_send,
@@ -221,57 +236,59 @@
     half = tok // 2
     head_dim = kv_ref.shape[1] // 2
     cols = hidden_mine.shape[1]
-    depth = w_ref.shape[0]
+    depth = x_proj_ref.shape[0]
     slab = out_ref.shape[0]
     piece = o_all.shape[1] // n_ctx
     repeat = piece * n_ctx // slab
 
-    def kv_slot(i, part):
-        if part is None:
-            return kv_all.at[pl.ds(pl.multiple_of(i * tok, tok), tok)]
-        return kv_all.at[pl.ds(pl.multiple_of(i * tok + part * half, half), half)]
-
-    def w_slot(i, part):
-        if part is None:
-            return w_all.at[pl.ds(pl.multiple_of(i * depth, depth), depth)]
-        return w_all.at[pl.ds(pl.multiple_of(i * depth + part * (depth // 2), depth // 2), depth // 2)]
+    def row_gather(index, own, everyone, first, count):
+        whole = own.shape[0]
+
+        def slot(i, part):
+            start, rows = (0, count) if part is None else (part * (count // 2), count // 2)
+            return everyone.at[pl.ds(pl.multiple_of(i * whole + (first + start), rows), rows)]
+
+        return RingGather(
+            own.at[pl.ds(first, count)],
+            slot,
+            n_ctx,
+            lambda part: own.at[pl.ds(first + part * (count // 2), count // 2)],
+            ring_send.at[index],
+            ring_recv.at[index],
+            local.at[index],
+        )
+
+    kv = row_gather(0, kv_ref, kv_all, 0, tok)
+    bc = row_gather(1, bc_proj_ref, bc_all, 0, depth)
+    chunk = depth // CHUNKS
+    xs = [row_gather(2 + i, x_proj_ref, x_all, i * chunk, chunk) for i in range(CHUNKS)]
+    weights = xs + [bc]
 
     def o_slot(i, part):
         rows = pl.ds(pl.multiple_of(i * piece, piece), piece)
         if part is None:
-            return o_all.at[:, rows]
-        return o_all.at[pl.ds(part * (n_tp // 2), n_tp // 2), rows]
-
-    kv = RingGather(
-        kv_ref, kv_slot, n_ctx, lambda part: kv_ref.at[pl.ds(part * half, half)],
-        kv_send, kv_recv, local.at[0],
-    )
-    w = RingGather(
-        w_ref, w_slot, n_ctx, lambda part: w_ref.at[pl.ds(part * (depth // 2), depth // 2)],
-        w_send, w_recv, local.at[1],
-    )
+            return o_all.at[pl.ds(1, n_tp - 1), rows]
+        return o_all.at[pl.ds(1, n_tp - 1), rows, pl.ds(part * (cols // 2), cols // 2)]
+
     o = RingGather(
         o_slot(ctx, None), o_slot, n_ctx, lambda part: o_slot(ctx, part),
-        o_send, o_recv, local.at[2],
+        ring_send.at[2 + CHUNKS], ring_recv.at[2 + CHUNKS], None,
     )
     barrier_with(
-        [{"ctx": to} for to in kv.neighbours()]
+        [{"ctx": (ctx + ahead) % n_ctx} for ahead in range(1, n_ctx)]
         + [{"tp": (tp + ahead) % n_tp} for ahead in range(1, n_tp)]
     )
 
     kv.start()
     my_rows = pl.ds(pl.multiple_of((ctx // repeat) * piece, piece), piece)
     my_place = pl.ds(pl.multiple_of(ctx * piece, piece), piece)
-
-    def o_columns(t):
-        return out_ref.at[my_rows, pl.ds(pl.multiple_of(t * cols, cols), cols)]
 
     swaps = []
     for ahead in range(1, n_tp):
         to = (tp + ahead) % n_tp
         swap = pltpu.make_async_remote_copy(
-            src_ref=o_columns(to),
-            dst_ref=o_all.at[tp, my_place],
+            src_ref=out_ref.at[my_rows, pl.ds(pl.multiple_of(to * cols, cols), cols)],
+            dst_ref=o_all.at[n_tp - ahead, my_place],
             send_sem=t_send.at[ahead],
             recv_sem=t_recv.at[ahead],
             device_id={"tp": to},
@@ -279,10 +296,13 @@
         )
         swap.start()
         swaps.append(swap)
-    keep_o = pltpu.make_async_copy(o_columns(tp), o_all.at[tp, my_place], local.at[3])
+    my_cols = pl.ds(pl.multiple_of(tp * cols, cols), cols)
+    keep_o = pltpu.make_async_copy(
+        out_ref.at[:, my_cols], o_all.at[0, pl.ds(0, slab)], local.at[2 + CHUNKS]
+    )
     keep_o.start()
     get_hidden = pltpu.make_async_copy(
-        hidden_ref.at[:, pl.ds(pl.multiple_of(tp * cols, cols), cols)], hidden_mine, local.at[4]
+        hidden_ref.at[:, my_cols], hidden_mine, local.at[3 + CHUNKS]
     )
     get_hidden.start()
 
@@ -297,15 +317,20 @@
 
     for step in range(1, kv.steps + 1):
         kv.step(step)
-
-    for ahead, swap in zip(range(1, n_tp), swaps):
-        swap.wait_recv()
-    keep_o.wait()
-    for way, to in ((0, o.right), (1, o.left)):
-        place = o_slot(ctx, o.part(1, way))
-        o.go(o.copy(place, place, o.ring_sem(1, way), to))
-    place = o_slot(ctx, None)
-    o.go(o.copy(place, place, 2 * o.steps, o.partner))
+    xs[0].start()
+    dt_all[ctx] = dt_proj_ref[...]
+    dts = []
+    for ahead in range(1, n_ctx):
+        copy = pltpu.make_async_remote_copy(
+            src_ref=dt_proj_ref,
+            dst_ref=dt_all.at[ctx],
+            send_sem=d_send.at[ahead],
+            recv_sem=d_recv.at[ahead],
+            device_id={"ctx": (ctx + ahead) % n_ctx},
+            device_id_type=MESH,
+        )
+        copy.start()
+        dts.append(copy)
     kv.finish()
 
     scale = 1.0 / math.sqrt(head_dim)
@@ -341,15 +366,19 @@
 
     lax.fori_loop(0, n_ctx, early_scores, 0)
     lax.fori_loop(0, n_ctx + 1, mixed_scores, 0)
-    o.step(1)
+
+    for swap in swaps:
+        swap.wait_recv()
+    o.start()
+    xs[1].start()
     for part in range(2):
         top[part] = jnp.broadcast_to(jnp.max(top[part], axis=1, keepdims=True), (rows, half))
 
     def add_block(slot, part, start):
-        weights = jnp.exp(scores[slot] - top[part])
-        total[part] = total[part] + weights
+        found = jnp.exp(scores[slot] - top[part])
+        total[part] = total[part] + found
         values = kv_all[pl.ds(pl.multiple_of(start, half), half), head_dim:]
-        mixed[part] = mixed[part] + jnp.dot(weights.astype(BF16), values, preferred_element_type=F32)
+        mixed[part] = mixed[part] + jnp.dot(found.astype(BF16), values, preferred_element_type=F32)
 
     def early_values(j, carry):
         add_block(j, 1, j * tok)
@@ -371,42 +400,75 @@
 
     attended = LineGather(att_all, n_tp, a_send, a_recv)
     attended.launch(1)
-    for step in range(2, o.steps + 1):
-        o.step(step)
-    w.start()
+    errands = [
+        lambda: o.step(1),
+        lambda: (xs[0].step(1), xs[2].start()),
+        lambda: (xs[1].step(1), xs[3].start()),
+    ]
+    errands += [functools.partial(o.step, step) for step in range(2, o.steps + 1)]
+    for at, step in enumerate(range(1, n_tp - 1)):
+        attended.arrive(step)
+        if at < 2:
+            errands.pop(0)()
+    while errands:
+        errands.pop(0)()
+    bc.start()
     get_hidden.wait()
-    other = 1 - o.core
-    place = o_slot(o.chip_at(0) * 2 + other, None)
-    o.copy(place, place, 2 * o.steps, o.partner).wait_recv()
-    for step in range(1, o.steps + 1):
-        for way in (0, 1):
-            ahead = o.chips - step if way == 0 else step
-            place = o_slot(o.chip_at(ahead) * 2 + other, o.part(step, way))
-            o.copy(place, place, o.pair_sem(step, way), o.partner).wait_recv()
+    keep_o.wait()
+    sums[...] = jnp.zeros_like(sums)
+
+    def add_heads(t):
+        slot = (t - tp + n_tp) % n_tp
+        weight = o_full[slot] if repeat > 1 else o_all[slot]
+        part = jnp.dot(att_all[t], weight, preferred_element_type=F32)
+        sums[...] += part.astype(BF16).astype(F32)
+
+    o.finish()
     if repeat > 1:
+        o_full[0] = o_all[0, :slab]
         for i in range(slab // piece):
-            o_full[:, i * piece : (i + 1) * piece] = o_all[:, i * repeat * piece : (i * repeat + 1) * piece]
-    weight = o_full if repeat > 1 else o_all
-
-    sums[...] = jnp.zeros_like(sums)
-
-    def add_heads(t):
-        part = jnp.dot(att_all[t], weight[t], preferred_element_type=F32)
-        sums[...] += part.astype(BF16).astype(F32)
-
+            o_full[1:, i * piece : (i + 1) * piece] = o_all[
+                1:, i * repeat * piece : (i * repeat + 1) * piece
+            ]
     add_heads(tp)
-    attended.run(add_heads)
+    for step in range(1, n_tp - 1):
+        attended.use(step, add_heads)
+    attended.arrive(n_tp - 1)
+    attended.use(n_tp - 1, add_heads)
     mine = (hidden_mine[...].astype(F32) + sums[...]).astype(BF16)
     res_ref[...] = mine
     res_all[tp] = mine
     residual = LineGather(res_all, n_tp, r_send, r_recv)
     residual.launch(1)
 
-    for step in range(1, w.steps + 1):
-        w.step(step)
-    w.finish()
-    proj[...] = jnp.zeros_like(proj)
+    errands = []
+    for step in range(2, bc.steps + 1):
+        errands.append(lambda step=step: (xs[0].step(step), xs[1].step(step)))
+    errands.append(lambda: xs[2].step(1))
+    errands.append(lambda: xs[3].step(1))
+    for step in range(2, bc.steps + 1):
+        errands.append(lambda step=step: xs[2].step(step))
+    errands.append(lambda: bc.step(1))
+    for step in range(2, bc.steps + 1):
+        errands.append(lambda step=step: xs[3].step(step))
+    for step in range(2, bc.steps + 1):
+        errands.append(lambda step=step: bc.step(step))
+    share_of = -(-len(errands) // max(1, n_tp - 1))
+    x_sum[...] = jnp.zeros_like(x_sum)
+    bc_sum[...] = jnp.zeros_like(bc_sum)
+    dt_sum[...] = jnp.zeros_like(dt_sum)
     square[...] = jnp.zeros_like(square)
+    for step in range(1, n_tp - 1):
+        for errand in errands[:share_of]:
+            errand()
+        errands = errands[share_of:]
+        residual.arrive(step)
+    for errand in errands:
+        errand()
+    for ahead, copy in enumerate(dts, 1):
+        copy.wait_recv()
+    for weight in weights:
+        weight.finish()
 
     def add_features(t):
         part = res_all[t].astype(F32)
@@ -416,31 +478,41 @@
             folded = folded + squares[:, i * LANES : (i + 1) * LANES]
         square[...] += folded
         scaled = (part * gain_ref[t]).astype(BF16)
-        proj[...] += jnp.dot(
-            scaled,
-            w_all[pl.ds(pl.multiple_of(t * cols, cols), cols), :],
-            preferred_element_type=F32,
-        )
+        at = pl.ds(pl.multiple_of(t * cols, cols), cols)
+        x_sum[...] += jnp.dot(scaled, x_all[at, :], preferred_element_type=F32)
+        bc_sum[...] += jnp.dot(scaled, bc_all[at, :], preferred_element_type=F32)
+        shards = cols // depth
+        for i in range(shards):
+            dt_sum[...] += lax.dot_general(
+                scaled[:, i * depth : (i + 1) * depth], dt_all[t * shards + i],
+                (((1,), (1,)), ((), ())), preferred_element_type=F32,
+            )
 
     add_features(tp)
-    residual.run(add_features)
+    for step in range(1, n_tp - 1):
+        residual.use(step, add_features)
+    residual.arrive(n_tp - 1)
+    residual.use(n_tp - 1, add_features)
     mean = jnp.sum(square[...], axis=1, keepdims=True) / (cols * n_tp)
     inverse = lax.rsqrt(mean + 1e-05)
-    x_wide, bc_wide = widths
-    x_ref[...] = (proj[:, :x_wide] * inverse).astype(BF16)
-    bc_ref[...] = (proj[:, x_wide : x_wide + bc_wide] * inverse).astype(BF16)
-    dt_ref[...] = proj[:, x_wide + bc_wide :] * inverse
-
-    kv.drain()
-    o.drain()
-    w.drain()
-    for swap in swaps:
-        swap.wait_send()
+    x_low[...] = (x_sum[...] * inverse).astype(BF16)
+    bc_low[...] = (bc_sum[...] * inverse).astype(BF16)
+    dt = dt_sum[...] * inverse
+    dt = jnp.concatenate([dt, jnp.zeros((tok, LANES - dt.shape[1]), F32)], axis=1)
+    mixer(n_ctx, m_local, x_low, bc_low, dt, bias_ref, log_ref, skip_ref, y_ref, *mixer_scratch)
+
+    for gather in [kv, o] + weights:
+        gather.drain()
+    for copy in swaps + dts:
+        copy.wait_send()
     attended.drain()
     residual.drain()
 
 
-def front(n_ctx, n_tp, queries, kv, hidden, out_proj, gain, weights, widths):
+def run_kernel(
+    n_ctx, n_tp, queries, kv, hidden, out_proj, gain, x_proj, bc_proj, dt_proj, bias, logs, skip,
+    m_local,
+):
     tok, q_wide = queries.shape
     head_dim = kv.shape[1] // 2
     heads = q_wide // head_dim
@@ -454,21 +526,24 @@
     line = 2 * (n_tp - 1)
     vmem = pl.BlockSpec(memory_space=pltpu.VMEM)
     hbm = pl.BlockSpec(memory_space=pl.ANY)
-    wide = weights.shape[1]
+    depth, wide = x_proj.shape
+    bc_wide = bc_proj.shape[1]
+    state = bc_wide // 2
+    share = wide // n_ctx
     dma = pltpu.SemaphoreType.DMA
     return pl.pallas_call(
-        functools.partial(front_kernel, n_ctx, n_tp, heads, widths),
+        functools.partial(whole_kernel, n_ctx, n_tp, heads, m_local),
         out_shape=(
             jax.ShapeDtypeStruct((tok, cols), BF16),
-            jax.ShapeDtypeStruct((tok, widths[0]), BF16),
-            jax.ShapeDtypeStruct((tok, widths[1]), BF16),
-            jax.ShapeDtypeStruct((tok, wide - widths[0] - widths[1]), F32),
+            jax.ShapeDtypeStruct((tok, wide), BF16),
         ),
-        in_specs=[vmem, vmem, hbm, hbm, vmem, hbm],
-        out_specs=(vmem,) * 4,
+        in_specs=[vmem, vmem, hbm, hbm, vmem, hbm, hbm, vmem, vmem, vmem, vmem],
+        out_specs=(vmem,) * 2,
         scratch_shapes=[
             pltpu.VMEM((n_ctx * tok, 2 * head_dim), BF16),
-            pltpu.VMEM((n_ctx * weights.shape[0], wide), BF16),
+            pltpu.VMEM((n_ctx * depth, wide), BF16),
+            pltpu.VMEM((n_ctx * depth, bc_wide), BF16),
+            pltpu.VMEM((n_ctx,) + dt_proj.shape, BF16),
             pltpu.VMEM((n_tp, n_ctx * piece, cols), BF16),
             pltpu.VMEM((n_tp, slab, cols) if repeat > 1 else (1, 16, LANES), BF16),
             pltpu.VMEM((n_tp, tok, q_wide), BF16),
@@ -481,25 +556,42 @@
             pltpu.VMEM((2, rows, head_dim), F32),
             pltpu.VMEM((tok, cols), F32),
             pltpu.VMEM((tok, wide), F32),
+            pltpu.VMEM((tok, bc_wide), F32),
+            pltpu.VMEM((tok, dt_proj.shape[0]), F32),
             pltpu.VMEM((tok, LANES), F32),
-            dma((ring,)),
-            dma((ring,)),
-            dma((ring,)),
-            dma((ring,)),
-            dma((ring,)),
-            dma((ring,)),
+            pltpu.VMEM((tok, wide), BF16),
+            pltpu.VMEM((tok, bc_wide), BF16),
+            [
+                pltpu.VMEM((n_ctx, 2 * share, state), BF16),
+                pltpu.VMEM((n_ctx, 2 * share, state), BF16),
+                pltpu.VMEM((8, LANES), F32),
+                pltpu.VMEM((n_ctx, 8, LANES), F32),
+                pltpu.VMEM((n_ctx, 2 * share, state), BF16),
+                pltpu.VMEM((n_ctx, 2 * share, state), BF16),
+                pltpu.VMEM((wide, state), F32),
+                pltpu.VMEM((tok, wide), F32),
+                pltpu.VMEM((tok, wide), F32),
+            ]
+            + [dma((n_ctx,))] * 6,
+            dma((3 + CHUNKS, ring)),
+            dma((3 + CHUNKS, ring)),
             dma((n_tp,)),
             dma((n_tp,)),
+            dma((n_ctx,)),
+            dma((n_ctx,)),
             dma((line,)),
             dma((line,)),
             dma((line,)),
             dma((line,)),
-            dma((5,)),
+            dma((4 + CHUNKS,)),
         ],
         compiler_params=pltpu.CompilerParams(
             collective_id=0, has_side_effects=True, vmem_limit_bytes=56 * 1024 * 1024
         ),
-    )(queries, kv, hidden, out_proj, gain.reshape(n_tp, 1, cols), weights)
+    )(
+        queries, kv, hidden, out_proj, gain.reshape(n_tp, 1, cols), x_proj, bc_proj, dt_proj,
+        bias, logs, skip,
+    )
 
 
 def exact_dot(a, b, dims):
@@ -508,12 +600,12 @@
     )
 
 
-def mixer_kernel(
+def mixer(
     n_ctx,
     m_local,
     x_ref,
     bc_ref,
-    dt_ref,
+    dt,
     bias_ref,
     log_ref,
     skip_ref,
@@ -540,7 +632,6 @@
     state = bc_ref.shape[1] // 2
     head_wide = wide // m_local
     share = wide // n_ctx
-    barrier_with([{"ctx": (me + ahead) % n_ctx} for ahead in range(1, n_ctx)])
 
     spread = (
         lax.broadcasted_iota(jnp.int32, (LANES, wide), 1) // head_wide
@@ -555,7 +646,7 @@
     log_out[...] = jnp.zeros_like(log_out)
     for chunk in range(2):
         at = slice(chunk * half, (chunk + 1) * half)
-        steps = jax.nn.softplus(dt_ref[at, :] + bias_ref[...])
+        steps = jax.nn.softplus(dt[at] + bias_ref[...])
         cumul = exact_dot(lower, steps * rates, ((1,), (0,)))
         last = cumul[half - 1 : half, :]
         log_out[chunk : chunk + 1, :] = last
@@ -653,35 +744,6 @@
         y_ref[at, :] = (inner[at, :] + grown[at, :] * carried).astype(BF16)
     for copy in copies:
         copy.wait_send()
-
-
-def mixer(n_ctx, m_local, x, bc, dt, bias, logs, skip):
-    tok, wide = x.shape
-    state = bc.shape[1] // 2
-    share = wide // n_ctx
-    vmem = pl.BlockSpec(memory_space=pltpu.VMEM)
-    dma = pltpu.SemaphoreType.DMA
-    return pl.pallas_call(
-        functools.partial(mixer_kernel, n_ctx, m_local),
-        out_shape=jax.ShapeDtypeStruct((tok, wide), BF16),
-        in_specs=[vmem] * 6,
-        out_specs=vmem,
-        scratch_shapes=[
-            pltpu.VMEM((n_ctx, 2 * share, state), BF16),
-            pltpu.VMEM((n_ctx, 2 * share, state), BF16),
-            pltpu.VMEM((8, LANES), F32),
-            pltpu.VMEM((n_ctx, 8, LANES), F32),
-            pltpu.VMEM((n_ctx, 2 * share, state), BF16),
-            pltpu.VMEM((n_ctx, 2 * share, state), BF16),
-            pltpu.VMEM((wide, state), F32),
-            pltpu.VMEM((tok, wide), F32),
-            pltpu.VMEM((tok, wide), F32),
-        ]
-        + [dma((n_ctx,))] * 6,
-        compiler_params=pltpu.CompilerParams(
-            collective_id=1, has_side_effects=True, vmem_limit_bytes=32 * 1024 * 1024
-        ),
-    )(x, bc, dt, bias, logs, skip)
 
 
 def body(
@@ -716,17 +778,16 @@
         axis=1,
     )
     bc_mine = lax.dynamic_index_in_dim(bc_proj, tp * m_local // per_group, 1, False)
+    rows = -(-m_local // 16) * 16
+    dt_mine = jnp.pad(dt_proj.T, ((0, rows - m_local), (0, 0)))
     pad = LANES - m_local
-    weights = jnp.concatenate([x_proj, bc_mine, jnp.pad(dt_proj, ((0, 0), (0, pad)))], axis=1)
-    widths = (x_proj.shape[1], bc_mine.shape[1])
-    residual_out, x, bc, dt = front(
-        n_ctx, n_tp, queries, kv, hidden, out_proj, norm_gain, weights, widths
-    )
     bias = jnp.pad(dt_bias, (0, pad)).reshape(1, LANES)
     logs = jnp.pad(decay_log, (0, pad)).reshape(1, LANES)
     skip = jnp.repeat(skip_gain, x_proj.shape[1] // m_local).reshape(1, -1)
-    mamba_out = mixer(n_ctx, m_local, x, bc, dt, bias, logs, skip)
-    return (residual_out, mamba_out)
+    return run_kernel(
+        n_ctx, n_tp, queries, kv, hidden, out_proj, norm_gain, x_proj, bc_mine, dt_mine,
+        bias, logs, skip, m_local,
+    )
 
 
 def solution(mesh):

time: 146 us -> 117 us (0.80)
  Pallas kernels: 133 us -> 106 us
  other arithmetic: 3.14 us -> 0.67 us
    pallas_call x2 -> x1, Pallas kernels: 133 us -> 106 us  [run_kernel(): pl.pallas_call(functools.partial(whole_kernel, n_ctx, n_tp, heads, m_loca...]
    unnamed x24 -> x7, local copies, waits for them, and re-layouts: 7.62 us -> 4.51 us
    concatenate x1 -> x0, other arithmetic: 2.47 us -> none  [body(): jnp.concatenate([x_proj, bc_mine, jnp.pad(dt_proj, ((0, 0), (0, pad)))],...]
where the time goes in v2:
time: 117 us; the launch traced here: 116 us
  Pallas kernels  106 us (91%)
  local copies, waits for them, and re-layouts  9.09 us (8%)
    pallas_call x1, Pallas kernels, run_kernel(): pl.pallas_call(functools.partial(whole_kernel, n_ctx, n_tp, heads, m_loca...  106 us
    unnamed x7, local copies, waits for them, and re-layouts  4.51 us

profile of v2, /device:TPU:1, one launch (start us, length us, event | category | flops | bytes accessed | tf_op | source)
XLA Modules:
  0.0 116.4 jit_solution(17606608658986888153)
XLA Ops:
  0.6 0.0 copy-start
  0.7 1.3 %pad_bitcast_fusion = (f32[1,128]{1,0:T(1,128)}, f32[1,128]{1,0:T(1,128)}) fusion(f32[16]{0:T(128)} %param.22, f32[16]{0:T(128)} %param.21), kind=kLoop, calls=%fused_computation.7 | loop fusion | bytes 1152 | tf_op jit(solution)/shard_map/reshape | solution.py:785
  2.0 0.7 broadcast_in_dim.3
  2.7 0.7 reshape_reshape.3.skip_ref
  3.4 1.3 %constant_dynamic-slice_fusion.1 = (bf16[256,1,128]{2,1,0:T(2,128)(2,1)S(1)}, bf16[256,1,128]{2,1,0:T(2,128)(2,1)S(1)}) fusion(bf16[256,4,128]{2,1,0:T(4,128)(2,1)} %param.14, s32[]{:T(128)S(6)} %select_n.18, bf16[256,4,128]{2,1,0:T(4,128)(2,1)} %param.13), kind=kLoop, calls=%fused_computation.5 | loop fusion | bytes 262148 | tf_op jit(solution)/shard_map/jit(dynamic_index_in_dim)/dynamic_slice | solution.py:776
  4.8 0.7 pad_maximum_fusion.kv_ref
  5.4 0.0 copy-done
  5.4 0.5 constant_dynamic-slice_fusion
  6.0 0.7 copy.23
  6.7 106.0 %shard_map.131 = (bf16[256,1024]{1,0:T(8,128)(2,1)}, bf16[256,1024]{1,0:T(8,128)(2,1)}) custom-call(bf16[256,512]{1,0:T(8,128)(2,1)} %q_ref.1, bf16[256,256]{1,0:T(8,128)(2,1)} %pad_maximum_fusion.kv_ref, bf16[256,4096]{1,0:T(8,128)(2,1)} %hidden_ref.1, bf16[512,4096]{1,0:T(8,128)(2,1)} %out_ref.1, f32[4,1,1024]{2,1,0:T(1,128)} %bitcast.18, ...), custom_call_target="tpu_custom_call" | custom-call | tf_op jit(solution)/shard_map/pallas_call | solution.py:534
  112.7 1.9 %copy.28 = bf16[256,1024]{1,0:T(8,128)(2,1)} copy(bf16[256,1024]{1,0:T(8,128)(2,1)} %get-tuple-element.8) | data formatting | bytes 1048576
  114.6 1.9 %copy.29 = bf16[256,1024]{1,0:T(8,128)(2,1)} copy(bf16[256,1024]{1,0:T(8,128)(2,1)} %get-tuple-element.9) | data formatting | bytes 1048576
  (2 shorter events, 0.0 us)
Async XLA Ops:
  0.6 4.8 %copy-start = (bf16[512,4,256]{2,1,0:T(4,128)(2,1)S(1)}, bf16[512,4,256]{2,1,0:T(4,128)(2,1)}, u32[]{:S(2)}) copy-start(bf16[512,4,256]{2,1,0:T(4,128)(2,1)} %param.19) | copy-start | bytes 3145732

commit v3 on v2

--- a/solution.py
+++ b/solution.py
@@ -86,18 +86,28 @@
                 self.go(self.copy(passed, passed, self.ring_sem(step + 1, way), to))
             self.go(self.copy(place, place, self.pair_sem(step, way), self.partner))
 
+    def other_own(self):
+        shard = self.chip_at(0) * 2 + 1 - self.core
+        place = self.slot(shard, None)
+        self.copy(place, place, 2 * self.steps, self.partner).wait_recv()
+
+    def other_step(self, step):
+        for way in (0, 1):
+            ahead = self.chips - step if way == 0 else step
+            shard = self.chip_at(ahead) * 2 + 1 - self.core
+            place = self.slot(shard, self.part(step, way))
+            self.copy(place, place, self.pair_sem(step, way), self.partner).wait_recv()
+
+    def shards(self, step, core):
+        far = [self.chip_at(self.chips - step), self.chip_at(step)]
+        return [chip * 2 + core for chip in (far if step < self.steps else far[:1])]
+
     def finish(self):
         if self.local is not None:
             self.keep.wait()
-        other = 1 - self.core
-        place = self.slot(self.chip_at(0) * 2 + other, None)
-        self.copy(place, place, 2 * self.steps, self.partner).wait_recv()
+        self.other_own()
         for step in range(1, self.steps + 1):
-            for way in (0, 1):
-                ahead = self.chips - step if way == 0 else step
-                shard = self.chip_at(ahead) * 2 + other
-                place = self.slot(shard, self.part(step, way))
-                self.copy(place, place, self.pair_sem(step, way), self.partner).wait_recv()
+            self.other_step(step)
 
     def drain(self):
         for copy in self.sent:
@@ -105,14 +115,14 @@
 
 
 class LineGather:
-    def __init__(self, buffer, n_tp, send, recv):
-        self.buffer, self.n_tp, self.send, self.recv = buffer, n_tp, send, recv
+    def __init__(self, buffer, part, n_tp, send, recv):
+        self.buffer, self.part, self.n_tp, self.send, self.recv = buffer, part, n_tp, send, recv
         self.me = lax.axis_index("tp")
 
     def copy(self, index, step, way, to):
         return pltpu.make_async_remote_copy(
-            src_ref=self.buffer.at[index],
-            dst_ref=self.buffer.at[index],
+            src_ref=self.buffer.at[index, self.part],
+            dst_ref=self.buffer.at[index, self.part],
             send_sem=self.send.at[2 * (step - 1) + way],
             recv_sem=self.recv.at[2 * (step - 1) + way],
             device_id={"tp": to},
@@ -315,9 +325,45 @@
     total[...] = jnp.zeros_like(total)
     mixed[...] = jnp.zeros_like(mixed)
 
-    for step in range(1, kv.steps + 1):
+    scale = 1.0 / math.sqrt(head_dim)
+    rows = heads * half
+    row_at = lax.broadcasted_iota(jnp.int32, (rows, half), 0) % half
+    col_at = lax.broadcasted_iota(jnp.int32, (rows, half), 1)
+    causal = col_at <= row_at
+
+    def late_of(shard):
+        return (shard - ctx - 1 + n_ctx) // n_ctx
+
+    def block_scores(keys_of, slot, part, start, masked):
+        keys = keys_of[pl.ds(pl.multiple_of(start, half), half), :head_dim]
+        found = lax.dot_general(
+            q_rows[part], keys, (((1,), (1,)), ((), ())), preferred_element_type=F32
+        ) * scale
+        if masked:
+            found = jnp.where(causal, found, -1e30)
+        scores[slot] = found
+        top[part] = jnp.maximum(top[part], found)
+
+    def shard_scores(shard):
+        block_scores(kv_all, shard, 1, shard * tok, False)
+        late = late_of(shard)
+        block_scores(kv_all, n_ctx + shard, late, shard * tok + late * half, False)
+
+    block_scores(kv_ref, ctx, 1, 0, False)
+    block_scores(kv_ref, n_ctx + ctx, 0, 0, True)
+    block_scores(kv_ref, 2 * n_ctx, 1, half, True)
+    kv.step(1)
+    kv.other_own()
+    shard_scores(kv.partner)
+    for shard in kv.shards(1, kv.core):
+        shard_scores(shard)
+    for step in range(2, kv.steps + 1):
         kv.step(step)
-    xs[0].start()
+        if step == 2:
+            xs[0].start()
+        kv.other_step(step - 1)
+        for shard in kv.shards(step - 1, 1 - kv.core) + kv.shards(step, kv.core):
+            shard_scores(shard)
     dt_all[ctx] = dt_proj_ref[...]
     dts = []
     for ahead in range(1, n_ctx):
@@ -331,46 +377,14 @@
         )
         copy.start()
         dts.append(copy)
-    kv.finish()
-
-    scale = 1.0 / math.sqrt(head_dim)
-    rows = heads * half
-    row_at = lax.broadcasted_iota(jnp.int32, (rows, half), 0) % half
-    col_at = lax.broadcasted_iota(jnp.int32, (rows, half), 1)
-    causal = col_at <= row_at
-
-    def place_of(unit):
-        late = (unit - ctx - 1 + n_ctx) // n_ctx
-        shard = unit - late
-        return late, shard, shard * tok + late * half
-
-    def block_scores(part, start):
-        keys = kv_all[pl.ds(pl.multiple_of(start, half), half), :head_dim]
-        return lax.dot_general(
-            q_rows[part], keys, (((1,), (1,)), ((), ())), preferred_element_type=F32
-        ) * scale
-
-    def early_scores(j, carry):
-        found = block_scores(1, j * tok)
-        scores[j] = found
-        top[1] = jnp.maximum(top[1], found)
-        return carry
-
-    def mixed_scores(unit, carry):
-        late, shard, start = place_of(unit)
-        found = block_scores(late, start)
-        found = jnp.where(causal | (shard != ctx), found, -1e30)
-        scores[n_ctx + unit] = found
-        top[late] = jnp.maximum(top[late], found)
-        return carry
-
-    lax.fori_loop(0, n_ctx, early_scores, 0)
-    lax.fori_loop(0, n_ctx + 1, mixed_scores, 0)
+    kv.other_step(kv.steps)
+    for shard in kv.shards(kv.steps, 1 - kv.core):
+        shard_scores(shard)
+    kv.keep.wait()
 
     for swap in swaps:
         swap.wait_recv()
     o.start()
-    xs[1].start()
     for part in range(2):
         top[part] = jnp.broadcast_to(jnp.max(top[part], axis=1, keepdims=True), (rows, half))
 
@@ -380,34 +394,44 @@
         values = kv_all[pl.ds(pl.multiple_of(start, half), half), head_dim:]
         mixed[part] = mixed[part] + jnp.dot(found.astype(BF16), values, preferred_element_type=F32)
 
-    def early_values(j, carry):
+    def early_early(j, carry):
+        add_block(n_ctx + j, 0, j * tok)
+        return carry
+
+    def late_early(j, carry):
         add_block(j, 1, j * tok)
         return carry
 
-    def mixed_values(unit, carry):
-        late, shard, start = place_of(unit)
-        add_block(n_ctx + unit, late, start)
+    def late_late(j, carry):
+        add_block(n_ctx + j, 1, j * tok + half)
         return carry
 
-    lax.fori_loop(0, n_ctx, early_values, 0)
-    lax.fori_loop(0, n_ctx + 1, mixed_values, 0)
-    for part in range(2):
+    def attend(part):
         ended = (mixed[part] / jnp.sum(total[part], axis=1, keepdims=True)).astype(BF16)
         for head in range(heads):
-            att_all[
-                tp, part * half : (part + 1) * half, head * head_dim : (head + 1) * head_dim
-            ] = ended[head * half : (head + 1) * half]
-
-    attended = LineGather(att_all, n_tp, a_send, a_recv)
-    attended.launch(1)
+            att_all[tp, part, :, head * head_dim : (head + 1) * head_dim] = ended[
+                head * half : (head + 1) * half
+            ]
+
+    attended = [LineGather(att_all, i, n_tp, a_send.at[i], a_recv.at[i]) for i in range(2)]
+    lax.fori_loop(0, ctx + 1, early_early, 0)
+    attend(0)
+    attended[0].launch(1)
+    lax.fori_loop(0, n_ctx, late_early, 0)
+    lax.fori_loop(ctx + 1, n_ctx, late_late, 0)
+    add_block(2 * n_ctx, 1, ctx * tok + half)
+    attend(1)
+    attended[1].launch(1)
+    xs[1].start()
     errands = [
         lambda: o.step(1),
-        lambda: (xs[0].step(1), xs[2].start()),
+        lambda: (xs[0].step(1), xs[2].start(), o.step(2)),
         lambda: (xs[1].step(1), xs[3].start()),
     ]
-    errands += [functools.partial(o.step, step) for step in range(2, o.steps + 1)]
+    errands += [functools.partial(o.step, step) for step in range(3, o.steps + 1)]
     for at, step in enumerate(range(1, n_tp - 1)):
-        attended.arrive(step)
+        attended[0].arrive(step)
+        attended[1].arrive(step)
         if at < 2:
             errands.pop(0)()
     while errands:
@@ -415,13 +439,12 @@
     bc.start()
     get_hidden.wait()
     keep_o.wait()
-    sums[...] = jnp.zeros_like(sums)
-
-    def add_heads(t):
+
+    def add_heads(t, part):
         slot = (t - tp + n_tp) % n_tp
         weight = o_full[slot] if repeat > 1 else o_all[slot]
-        part = jnp.dot(att_all[t], weight, preferred_element_type=F32)
-        sums[...] += part.astype(BF16).astype(F32)
+        found = jnp.dot(att_all[t, part], weight, preferred_element_type=F32)
+        sums[part] += found.astype(BF16).astype(F32)
 
     o.finish()
     if repeat > 1:
@@ -430,16 +453,20 @@
             o_full[1:, i * piece : (i + 1) * piece] = o_all[
                 1:, i * repeat * piece : (i * repeat + 1) * piece
             ]
-    add_heads(tp)
-    for step in range(1, n_tp - 1):
-        attended.use(step, add_heads)
-    attended.arrive(n_tp - 1)
-    attended.use(n_tp - 1, add_heads)
-    mine = (hidden_mine[...].astype(F32) + sums[...]).astype(BF16)
-    res_ref[...] = mine
-    res_all[tp] = mine
-    residual = LineGather(res_all, n_tp, r_send, r_recv)
-    residual.launch(1)
+    residual = [LineGather(res_all, i, n_tp, r_send.at[i], r_recv.at[i]) for i in range(2)]
+    sums[...] = jnp.zeros_like(sums)
+    for part in range(2):
+        take = functools.partial(add_heads, part=part)
+        take(tp)
+        for step in range(1, n_tp - 1):
+            attended[part].use(step, take)
+        attended[part].arrive(n_tp - 1)
+        attended[part].use(n_tp - 1, take)
+        at = slice(part * half, (part + 1) * half)
+        mine = (hidden_mine[at, :].astype(F32) + sums[part]).astype(BF16)
+        res_all[tp, part] = mine
+        residual[part].launch(1)
+        res_ref[at, :] = mine
 
     errands = []
     for step in range(2, bc.steps + 1):
@@ -462,7 +489,8 @@
         for errand in errands[:share_of]:
             errand()
         errands = errands[share_of:]
-        residual.arrive(step)
+        residual[0].arrive(step)
+        residual[1].arrive(step)
     for errand in errands:
         errand()
     for ahead, copy in enumerate(dts, 1):
@@ -471,7 +499,7 @@
         weight.finish()
 
     def add_features(t):
-        part = res_all[t].astype(F32)
+        part = res_all[t].reshape(tok, cols).astype(F32)
         squares = part * part
         folded = squares[:, :LANES]
         for i in range(1, cols // LANES):
@@ -490,9 +518,10 @@
 
     add_features(tp)
     for step in range(1, n_tp - 1):
-        residual.use(step, add_features)
-    residual.arrive(n_tp - 1)
-    residual.use(n_tp - 1, add_features)
+        residual[0].use(step, add_features)
+    residual[0].arrive(n_tp - 1)
+    residual[1].arrive(n_tp - 1)
+    residual[0].use(n_tp - 1, add_features)
     mean = jnp.sum(square[...], axis=1, keepdims=True) / (cols * n_tp)
     inverse = lax.rsqrt(mean + 1e-05)
     x_low[...] = (x_sum[...] * inverse).astype(BF16)
@@ -505,8 +534,8 @@
         gather.drain()
     for copy in swaps + dts:
         copy.wait_send()
-    attended.drain()
-    residual.drain()
+    for line in attended + residual:
+        line.drain()
 
 
 def run_kernel(
@@ -546,15 +575,15 @@
             pltpu.VMEM((n_ctx,) + dt_proj.shape, BF16),
             pltpu.VMEM((n_tp, n_ctx * piece, cols), BF16),
             pltpu.VMEM((n_tp, slab, cols) if repeat > 1 else (1, 16, LANES), BF16),
-            pltpu.VMEM((n_tp, tok, q_wide), BF16),
-            pltpu.VMEM((n_tp, tok, cols), BF16),
+            pltpu.VMEM((n_tp, 2, half, q_wide), BF16),
+            pltpu.VMEM((n_tp, 2, half, cols), BF16),
             pltpu.VMEM((tok, cols), BF16),
             pltpu.VMEM((2, rows, head_dim), BF16),
             pltpu.VMEM((2 * n_ctx + 1, rows, half), F32),
             pltpu.VMEM((2, rows, half), F32),
             pltpu.VMEM((2, rows, half), F32),
             pltpu.VMEM((2, rows, head_dim), F32),
-            pltpu.VMEM((tok, cols), F32),
+            pltpu.VMEM((2, half, cols), F32),
             pltpu.VMEM((tok, wide), F32),
             pltpu.VMEM((tok, bc_wide), F32),
             pltpu.VMEM((tok, dt_proj.shape[0]), F32),
@@ -579,10 +608,10 @@
             dma((n_tp,)),
             dma((n_ctx,)),
             dma((n_ctx,)),
-            dma((line,)),
-            dma((line,)),
-            dma((line,)),
-            dma((line,)),
+            dma((2, line)),
+            dma((2, line)),
+            dma((2, line)),
+            dma((2, line)),
             dma((4 + CHUNKS,)),
         ],
         compiler_params=pltpu.CompilerParams(
@@ -636,7 +665,16 @@
     spread = (
         lax.broadcasted_iota(jnp.int32, (LANES, wide), 1) // head_wide
         == lax.broadcasted_iota(jnp.int32, (LANES, wide), 0)
-    ).astype(F32)
+    ).astype(F32).astype(BF16)
+    spread = jnp.concatenate([spread, spread], axis=0)
+
+    def widen(values):
+        upper = values.astype(BF16)
+        lower = (values - upper.astype(F32)).astype(BF16)
+        return jnp.dot(
+            jnp.concatenate([upper, lower], axis=1), spread, preferred_element_type=F32
+        )
+
     across = lax.broadcasted_iota(jnp.int32, (half, half), 1)
     down = lax.broadcasted_iota(jnp.int32, (half, half), 0)
     causal = across <= down
@@ -650,14 +688,13 @@
         cumul = exact_dot(lower, steps * rates, ((1,), (0,)))
         last = cumul[half - 1 : half, :]
         log_out[chunk : chunk + 1, :] = last
-        tail = exact_dot(jnp.exp(last - cumul) * steps, spread, ((1,), (0,)))
+        tail = widen(jnp.exp(last - cumul) * steps)
         weighted = (x_ref[at, :].astype(F32) * tail).astype(BF16)
         made = lax.dot_general(
             weighted, bc_ref[at, :state], (((0,), (0,)), ((), ())), preferred_element_type=F32
         ).astype(BF16)
         for i in range(n_ctx):
             state_out[i, chunk * share : (chunk + 1) * share, :] = made[i * share : (i + 1) * share]
-        grown[at, :] = exact_dot(jnp.exp(cumul), spread, ((1,), (0,)))
         kept.append((cumul, steps))
 
     def transfer(src, dst, send, recv, ahead):
@@ -682,9 +719,11 @@
     state_in[me] = state_out[me]
     log_in[me] = log_out[...]
 
+    skip = widen(jnp.broadcast_to(skip_ref[...], (16, LANES)))[:1]
     for chunk in range(2):
         at = slice(chunk * half, (chunk + 1) * half)
         cumul, steps = kept[chunk]
+        grown[at, :] = widen(jnp.exp(cumul))
         cumul_t, steps_t = cumul.T, steps.T
         gram = lax.dot_general(
             bc_ref[at, state:], bc_ref[at, :state], (((1,), (1,)), ((), ())),
@@ -702,7 +741,7 @@
                 mixing = gram * jnp.exp(gap) * steps_t[head : head + 1, :]
                 one = jnp.dot(mixing.astype(BF16), x_pair, preferred_element_type=F32)
                 found = one if k == 0 else jnp.where(across // head_wide == k, one, found)
-            inner[at, lanes] = found + skip_ref[:, lanes] * x_pair.astype(F32)
+            inner[at, lanes] = found + skip[:, lanes] * x_pair.astype(F32)
 
     for ahead in range(1, n_ctx):
         src = (me + n_ctx - ahead) % n_ctx
@@ -783,7 +822,7 @@
     pad = LANES - m_local
     bias = jnp.pad(dt_bias, (0, pad)).reshape(1, LANES)
     logs = jnp.pad(decay_log, (0, pad)).reshape(1, LANES)
-    skip = jnp.repeat(skip_gain, x_proj.shape[1] // m_local).reshape(1, -1)
+    skip = jnp.pad(skip_gain, (0, pad)).reshape(1, LANES)
     return run_kernel(
         n_ctx, n_tp, queries, kv, hidden, out_proj, norm_gain, x_proj, bc_mine, dt_mine,
         bias, logs, skip, m_local,

time: 117 us -> 110 us (0.940)
  Pallas kernels: 106 us -> 99.4 us
    pallas_call x1, Pallas kernels: 106 us -> 99.4 us  [run_kernel(): pl.pallas_call(functools.partial(whole_kernel, n_ctx, n_tp, heads, m_loca...]
    reshape x1 -> x2, local copies, waits for them, and re-layouts: 1.34 us -> 2.48 us  [the longest x1 1.25 us: body(): skip = jnp.pad(skip_gain, (0, pad)).reshape(1, LANES)]
where the time goes in v3:
time: 110 us
  Pallas kernels  99.4 us (90%)
  local copies, waits for them, and re-layouts  8.83 us (8%)
    pallas_call x1, Pallas kernels, run_kernel(): pl.pallas_call(functools.partial(whole_kernel, n_ctx, n_tp, heads, m_loca...  99.4 us
    unnamed x7, local copies, waits for them, and re-layouts  4.51 us

profile of v3, /device:TPU:1, one launch (start us, length us, event | category | flops | bytes accessed | tf_op | source)
XLA Modules:
  0.0 109.6 jit_solution(2577415166253597662)
XLA Ops:
  0.6 0.0 copy-start
  0.7 1.2 %pad_bitcast_fusion.2.bias_ref = f32[1,128]{1,0:T(1,128)} fusion(f32[16]{0:T(128)} %param.21), kind=kLoop, calls=%fused_computation.9 | loop fusion | bytes 576 | tf_op jit(solution)/shard_map/reshape | solution.py:823
  1.9 1.3 %pad_bitcast_fusion = (f32[1,128]{1,0:T(1,128)}, f32[1,128]{1,0:T(1,128)}) fusion(f32[16]{0:T(128)} %param.23, f32[16]{0:T(128)} %param.22), kind=kLoop, calls=%fused_computation.7 | loop fusion | bytes 1152 | tf_op jit(solution)/shard_map/reshape | solution.py:825
  3.2 1.3 %constant_dynamic-slice_fusion.1 = (bf16[256,1,128]{2,1,0:T(2,128)(2,1)S(1)}, bf16[256,1,128]{2,1,0:T(2,128)(2,1)S(1)}) fusion(bf16[256,4,128]{2,1,0:T(4,128)(2,1)} %param.14, s32[]{:T(128)S(6)} %select_n.18, bf16[256,4,128]{2,1,0:T(4,128)(2,1)} %param.13), kind=kLoop, calls=%fused_computation.5 | loop fusion | bytes 262148 | tf_op jit(solution)/shard_map/jit(dynamic_index_in_dim)/dynamic_slice | solution.py:815
  4.5 0.7 pad_maximum_fusion.kv_ref
  5.2 0.0 copy-done
  5.2 0.5 constant_dynamic-slice_fusion
  5.7 0.7 copy.23
  6.5 99.4 %shard_map.131 = (bf16[256,1024]{1,0:T(8,128)(2,1)}, bf16[256,1024]{1,0:T(8,128)(2,1)}) custom-call(bf16[256,512]{1,0:T(8,128)(2,1)} %q_ref.1, bf16[256,256]{1,0:T(8,128)(2,1)} %pad_maximum_fusion.kv_ref, bf16[256,4096]{1,0:T(8,128)(2,1)} %hidden_ref.1, bf16[512,4096]{1,0:T(8,128)(2,1)} %out_ref.1, f32[4,1,1024]{2,1,0:T(1,128)} %bitcast.20, ...), custom_call_target="tpu_custom_call" | custom-call | tf_op jit(solution)/shard_map/pallas_call | solution.py:563
  105.9 1.9 %copy.28 = bf16[256,1024]{1,0:T(8,128)(2,1)} copy(bf16[256,1024]{1,0:T(8,128)(2,1)} %get-tuple-element.8) | data formatting | bytes 1048576
  107.7 1.9 %copy.29 = bf16[256,1024]{1,0:T(8,128)(2,1)} copy(bf16[256,1024]{1,0:T(8,128)(2,1)} %get-tuple-element.9) | data formatting | bytes 1048576
  (2 shorter events, 0.0 us)
Async XLA Ops:
  0.6 4.5 %copy-start = (bf16[512,4,256]{2,1,0:T(4,128)(2,1)S(1)}, bf16[512,4,256]{2,1,0:T(4,128)(2,1)}, u32[]{:S(2)}) copy-start(bf16[512,4,256]{2,1,0:T(4,128)(2,1)} %param.19) | copy-start | bytes 3145732

commit v4 on v3

--- a/solution.py
+++ b/solution.py
@@ -417,16 +417,17 @@
     lax.fori_loop(0, ctx + 1, early_early, 0)
     attend(0)
     attended[0].launch(1)
+    xs[0].step(1)
+    xs[1].start()
     lax.fori_loop(0, n_ctx, late_early, 0)
     lax.fori_loop(ctx + 1, n_ctx, late_late, 0)
     add_block(2 * n_ctx, 1, ctx * tok + half)
     attend(1)
     attended[1].launch(1)
-    xs[1].start()
+    xs[2].start()
     errands = [
-        lambda: o.step(1),
-        lambda: (xs[0].step(1), xs[2].start(), o.step(2)),
-        lambda: (xs[1].step(1), xs[3].start()),
+        lambda: (o.step(1), xs[3].start()),
+        lambda: (xs[1].step(1), o.step(2), bc.start()),
     ]
     errands += [functools.partial(o.step, step) for step in range(3, o.steps + 1)]
     for at, step in enumerate(range(1, n_tp - 1)):
@@ -436,7 +437,6 @@
             errands.pop(0)()
     while errands:
         errands.pop(0)()
-    bc.start()
     get_hidden.wait()
     keep_o.wait()
 
@@ -469,17 +469,19 @@
         res_ref[at, :] = mine
 
     errands = []
-    for step in range(2, bc.steps + 1):
-        errands.append(lambda step=step: (xs[0].step(step), xs[1].step(step)))
-    errands.append(lambda: xs[2].step(1))
-    errands.append(lambda: xs[3].step(1))
-    for step in range(2, bc.steps + 1):
-        errands.append(lambda step=step: xs[2].step(step))
-    errands.append(lambda: bc.step(1))
-    for step in range(2, bc.steps + 1):
-        errands.append(lambda step=step: xs[3].step(step))
-    for step in range(2, bc.steps + 1):
-        errands.append(lambda step=step: bc.step(step))
+
+    def later(gather, first, last):
+        for step in range(first, last + 1):
+            errands.append(functools.partial(gather.step, step))
+
+    for gather in xs[:2]:
+        later(gather, 2, gather.steps)
+    later(xs[2], 1, 1)
+    later(xs[3], 1, 1)
+    later(xs[2], 2, bc.steps)
+    later(bc, 1, 1)
+    later(xs[3], 2, bc.steps)
+    later(bc, 2, bc.steps)
     share_of = -(-len(errands) // max(1, n_tp - 1))
     x_sum[...] = jnp.zeros_like(x_sum)
     bc_sum[...] = jnp.zeros_like(bc_sum)
@@ -615,7 +617,7 @@
             dma((4 + CHUNKS,)),
         ],
         compiler_params=pltpu.CompilerParams(
-            collective_id=0, has_side_effects=True, vmem_limit_bytes=56 * 1024 * 1024
+            collective_id=0, has_side_effects=True, vmem_limit_bytes=42 * 1024 * 1024
         ),
     )(
         queries, kv, hidden, out_proj, gain.reshape(n_tp, 1, cols), x_proj, bc_proj, dt_proj,
@@ -679,12 +681,16 @@
     down = lax.broadcasted_iota(jnp.int32, (half, half), 0)
     causal = across <= down
     lower = causal.astype(F32)
-    rates = -jnp.exp(log_ref[...])
+
+    def padded(ref):
+        return jnp.concatenate([ref[...], jnp.zeros((1, LANES - m_local), F32)], axis=1)
+
+    bias, rates = padded(bias_ref), -jnp.exp(padded(log_ref))
     kept = []
     log_out[...] = jnp.zeros_like(log_out)
     for chunk in range(2):
         at = slice(chunk * half, (chunk + 1) * half)
-        steps = jax.nn.softplus(dt[at] + bias_ref[...])
+        steps = jax.nn.softplus(dt[at] + bias)
         cumul = exact_dot(lower, steps * rates, ((1,), (0,)))
         last = cumul[half - 1 : half, :]
         log_out[chunk : chunk + 1, :] = last
@@ -719,7 +725,7 @@
     state_in[me] = state_out[me]
     log_in[me] = log_out[...]
 
-    skip = widen(jnp.broadcast_to(skip_ref[...], (16, LANES)))[:1]
+    skip = widen(jnp.broadcast_to(padded(skip_ref), (16, LANES)))[:1]
     for chunk in range(2):
         at = slice(chunk * half, (chunk + 1) * half)
         cumul, steps = kept[chunk]
@@ -819,10 +825,7 @@
     bc_mine = lax.dynamic_index_in_dim(bc_proj, tp * m_local // per_group, 1, False)
     rows = -(-m_local // 16) * 16
     dt_mine = jnp.pad(dt_proj.T, ((0, rows - m_local), (0, 0)))
-    pad = LANES - m_local
-    bias = jnp.pad(dt_bias, (0, pad)).reshape(1, LANES)
-    logs = jnp.pad(decay_log, (0, pad)).reshape(1, LANES)
-    skip = jnp.pad(skip_gain, (0, pad)).reshape(1, LANES)
+    bias, logs, skip = (part.reshape(1, m_local) for part in (dt_bias, decay_log, skip_gain))
     return run_kernel(
         n_ctx, n_tp, queries, kv, hidden, out_proj, norm_gain, x_proj, bc_mine, dt_mine,
         bias, logs, skip, m_local,

time: 110 us -> 118 us (1.073)
  Pallas kernels: 99.4 us -> 105 us
  local copies, waits for them, and re-layouts: 8.83 us -> 11.4 us
    pallas_call x1, Pallas kernels: 99.4 us -> 105 us  [run_kernel(): pl.pallas_call(functools.partial(whole_kernel, n_ctx, n_tp, heads, m_loca...]
    unnamed x7 -> x25, local copies, waits for them, and re-layouts: 4.51 us -> 9.42 us
    reshape x2 -> x0, local copies, waits for them, and re-layouts: 2.48 us -> none  [the longest x1 1.25 us: body(): skip = jnp.pad(skip_gain, (0, pad)).reshape(1, LANES)]
where the time goes in v4:
time: 118 us
  Pallas kernels  105 us (89%)
  local copies, waits for them, and re-layouts  11.4 us (10%)
    pallas_call x1, Pallas kernels, run_kernel(): pl.pallas_call(functools.partial(whole_kernel, n_ctx, n_tp, heads, m_loca...  105 us
    unnamed x25, local copies, waits for them, and re-layouts  9.42 us

profile of v4, /device:TPU:1, one launch (start us, length us, event | category | flops | bytes accessed | tf_op | source)
XLA Modules:
  0.0 117.7 jit_solution(9785320566868362739)
XLA Ops:
  0.6 0.0 copy-start
  0.6 0.0 copy-start.2
  0.7 1.5 %constant_dynamic-slice_fusion.1 = (bf16[256,1,128]{2,1,0:T(2,128)(2,1)S(1)}, bf16[256,1,128]{2,1,0:T(2,128)(2,1)S(1)}) fusion(bf16[256,4,128]{2,1,0:T(4,128)(2,1)} %param.14, s32[]{:T(128)S(6)} %select_n.18, bf16[256,4,128]{2,1,0:T(4,128)(2,1)} %param.13), kind=kLoop, calls=%fused_computation.5 | loop fusion | bytes 262148 | tf_op jit(solution)/shard_map/jit(dynamic_index_in_dim)/dynamic_slice | solution.py:821
  2.2 0.0 copy-done
  2.2 0.5 constant_dynamic-slice_fusion
  2.8 0.0 copy-done.2
  2.8 0.0 copy-start.1
  2.9 2.2 %copy-done.1 = bf16[512,4096]{1,0:T(8,128)(2,1)S(1)} copy-done((bf16[512,4096]{1,0:T(8,128)(2,1)S(1)}, bf16[512,4096]{1,0:T(8,128)(2,1)}, u32[]{:S(2)}) %copy-start.1) | copy-done | bytes 4194328
  5.0 0.0 copy-start.3
  5.0 1.2 %copy-done.3 = bf16[512,1024]{1,0:T(8,128)(2,1)S(1)} copy-done((bf16[512,1024]{1,0:T(8,128)(2,1)S(1)}, bf16[512,1024]{1,0:T(8,128)(2,1)}, u32[]{:S(2)}) %copy-start.3) | copy-done | bytes 1048600
  6.3 0.0 copy-start.4
  6.3 0.9 copy-done.4
  7.2 0.0 copy-start.5
  7.2 0.7 copy-done.5
  7.9 0.0 copy-start.6
  7.9 0.7 copy-done.6
  8.6 0.0 copy-start.7
  8.6 0.7 copy-done.7
  9.3 0.0 copy-start.8
  9.3 0.7 copy-done.8
  10.0 0.0 copy-start.9
  10.0 0.7 copy-done.9
  10.6 105.5 %shard_map.131 = (bf16[256,1024]{1,0:T(8,128)(2,1)S(1)}, bf16[256,1024]{1,0:T(8,128)(2,1)S(1)}) custom-call(bf16[256,512]{1,0:T(8,128)(2,1)S(1)} %copy-done.4, bf16[256,256]{1,0:T(8,128)(2,1)S(1)} %pad_maximum_fusion.kv_ref, bf16[256,4096]{1,0:T(8,128)(2,1)S(1)} %copy-done.2, bf16[512,4096]{1,0:T(8,128)(2,1)S(1)} %copy-done.1, f32[4,1,1024]{2,1,0:T(1,128)S(1)} %bitcast.15, ...), custom_call_target="tpu_custom_call" | custom-call | tf_op jit(solution)/shard_map/pallas_call | solution.py:565
  116.1 0.8 copy.28
  116.9 0.8 copy.29
  (4 shorter events, 0.1 us)
Async XLA Ops:
  0.6 1.6 %copy-start = (bf16[512,4,256]{2,1,0:T(4,128)(2,1)S(1)}, bf16[512,4,256]{2,1,0:T(4,128)(2,1)}, u32[]{:S(2)}) copy-start(bf16[512,4,256]{2,1,0:T(4,128)(2,1)} %param.19) | copy-start | bytes 3145732
  0.6 2.2 %copy-start.2 = (bf16[256,4096]{1,0:T(8,128)(2,1)S(1)}, bf16[256,4096]{1,0:T(8,128)(2,1)}, u32[]{:S(2)}) copy-start(bf16[256,4096]{1,0:T(8,128)(2,1)} %hidden_ref.1) | copy-start | bytes 6291460
  2.8 2.2 %copy-start.1 = (bf16[512,4096]{1,0:T(8,128)(2,1)S(1)}, bf16[512,4096]{1,0:T(8,128)(2,1)}, u32[]{:S(2)}) copy-start(bf16[512,4096]{1,0:T(8,128)(2,1)} %out_ref.1) | copy-start | bytes 12582916
  5.0 1.2 %copy-start.3 = (bf16[512,1024]{1,0:T(8,128)(2,1)S(1)}, bf16[512,1024]{1,0:T(8,128)(2,1)}, u32[]{:S(2)}) copy-start(bf16[512,1024]{1,0:T(8,128)(2,1)} %x_proj_ref.1) | copy-start | bytes 3145732
  6.3 0.9 copy-start.4
  7.2 0.7 copy-start.5
  7.9 0.7 copy-start.6
  8.6 0.7 copy-start.7
  9.3 0.7 copy-start.8
  10.0 0.7 copy-start.9
